TPU v7x, 32 devices: a whole 2x2x4 slice. The times are simulated.
32 devices in a mesh: grp: 8 (over y, x, core), shard: 4 (over z).
Axes of the slice: x: 2, y: 2, z: 4, core: 2. Of those that a mesh axis runs over, the one named last changes fastest.
Arguments:
- tokens: bfloat16 [2, 8, 512, 2048], P(None, 'grp', 'shard'), may hold values from -6 to 6
- cotangent: bfloat16 [2, 8, 512, 2048], P(None, 'grp', 'shard'), may hold values from -6 to 6
- sequence_lengths: int32 [2, 8, 4], P(None, 'grp'), may hold values from 1 to 448, as said below
- attention_norm_gain: bfloat16 [2048], P('shard'), may hold values from 0.5 to 1.5
- query_matrix: bfloat16 [2048, 2048], P('shard'), may hold values from -0.125 to 0.125
- key_value_matrix: bfloat16 [2048, 1024], P('shard'), may hold values from -0.125 to 0.125
- output_matrix: bfloat16 [2048, 2048], P('shard'), may hold values from -0.375 to 0.375
- adapter_down_maps: bfloat16 [2048, 24], P('shard'), may hold values from -0.125 to 0.125
- adapter_up_query: bfloat16 [8, 2048], P(None, 'shard'), may hold values from -1 to 1
- adapter_up_key_value: bfloat16 [2, 8, 512], P(None, None, 'shard'), may hold values from -1 to 1
- adapter_down_output: bfloat16 [2048, 8], P('shard'), may hold values from -0.125 to 0.125
- adapter_up_output: bfloat16 [8, 2048], P(None, 'shard'), may hold values from -1 to 1
- query_feature_matrices: bfloat16 [32, 64, 64], P('shard'), may hold values from -1.5 to 1.5
- key_feature_matrices: bfloat16 [8, 64, 64], P('shard'), may hold values from -1.5 to 1.5
- feedforward_norm_gain: bfloat16 [2048], P('shard'), may hold values from 0.5 to 1.5
- gate_matrix: bfloat16 [2048, 8192], P('shard'), may hold values from -0.125 to 0.125
- up_matrix: bfloat16 [2048, 8192], P('shard'), may hold values from -0.125 to 0.125
- down_matrix: bfloat16 [8192, 2048], P('shard'), may hold values from -0.125 to 0.125
Outputs:
- output: bfloat16 [2, 8, 512, 2048], P(None, 'grp', 'shard')
- grad_tokens: bfloat16 [2, 8, 512, 2048], P(None, 'grp', 'shard')
- grad_attn_gain: float32 [2048], P('shard')
- grad_query_weight: float32 [2048, 2048], P('shard', 'grp')
- grad_keyvalue_weight: float32 [2048, 1024], P('shard', 'grp')
- grad_output_weight: float32 [2048, 2048], P('shard', 'grp')
- adapter_down_gradient: float32 [2048, 24], P('shard')
- adapter_up_query_gradient: float32 [8, 2048], P(None, 'shard')
- adapter_up_key_value_gradient: float32 [2, 8, 512], P(None, None, 'shard')
- adapter_down_output_gradient: float32 [2048, 8], P('shard')
- adapter_up_output_gradient: float32 [8, 2048], P(None, 'shard')
- grad_feature_query: float32 [32, 64, 64], P('shard')
- grad_feature_key: float32 [8, 64, 64], P('shard')
- grad_ffn_gain: float32 [2048], P('shard')
- grad_gate_weight: float32 [2048, 8192], P('shard', 'grp')
- grad_up_weight: float32 [2048, 8192], P('shard', 'grp')
- grad_down_weight: float32 [8192, 2048], P('shard', 'grp')
Inputs may be any that keep to these rules, and one draw needn't show every extreme that they name: `sequence_lengths`: each row lists 4 - 1 document lengths in order, then the padding slots at the stream's end (1 or more); the entries sum to 512, and one document of each row has exactly 448 tokens.
All inputs are finite; a program needn't handle non-finite values.
Results may differ from a plain program's by a relative error of at most 0.02.
Values may be sent and summed in bfloat16 or wider, within the bound.
No kernel may reach another device: no remote copies, remote signals or barrier semaphores. Data moves between devices by JAX's collectives and lax.ppermute only.
A program may use at most 768 MiB of HBM per device.

v0:
```python
import functools
import jax
import jax.numpy as jnp
from jax import lax
from jax.experimental import pallas as pl
from jax.experimental.pallas import tpu as pltpu
from jax.sharding import PartitionSpec as P

WIN = 64
EPS = 1e-05
ROPE_BASE = 500000.0
BF = jnp.bfloat16
F32 = jnp.float32
QB = 128


def nn(a, b):
    return lax.dot_general(a, b, (((1,), (0,)), ((), ())), preferred_element_type=F32)


def nt(a, b):
    return lax.dot_general(a, b, (((1,), (1,)), ((), ())), preferred_element_type=F32)


def tn(a, b):
    return lax.dot_general(a, b, (((0,), (0,)), ((), ())), preferred_element_type=F32)


def turned(x, cos, sin):
    half = x.shape[0] // 2
    a, b = x[:half], x[half:]
    return jnp.concatenate([a * cos - b * sin, b * cos + a * sin], axis=0)


def features(z):
    half = z.shape[0] // 2

    def one(part):
        e = jnp.exp(part - jnp.max(part, axis=0, keepdims=True))
        return e / jnp.sum(e, axis=0, keepdims=True)

    return jnp.concatenate([one(z[:half]), one(z[half:])], axis=0)


def features_back(p, g):
    half = p.shape[0] // 2

    def one(pp, gg):
        return pp * (gg - jnp.sum(pp * gg, axis=0, keepdims=True))

    return one(p[:half], g[:half]) - one(p[half:], g[half:])


def masks(drow_ref, dcol_ref, q0, k0, count, heads):
    same = dcol_ref[k0 : k0 + count, :] == drow_ref[0:1, q0 : q0 + QB]
    dist = (
        lax.broadcasted_iota(jnp.int32, (count, QB), 1)
        - lax.broadcasted_iota(jnp.int32, (count, QB), 0)
        + (q0 - k0)
    )
    window = jnp.where(same & (dist >= 0) & (dist < WIN), 1.0, 0.0)
    linear = jnp.where(same & (dist >= WIN), 1.0, 0.0)
    return (
        jnp.concatenate([window] * heads, axis=1),
        jnp.concatenate([linear] * heads, axis=1),
    )


def side(parts):
    return jnp.concatenate(parts, axis=1)


def mixed_rows(win_part, lin_part, w0, l1, n):
    pieces = []
    if w0 > 0:
        pieces.append(lin_part[:w0])
    pieces.append(lin_part[w0:l1] + win_part[: l1 - w0])
    pieces.append(win_part[l1 - w0 :])
    return jnp.concatenate(pieces, axis=0)


def block_pick(me_ref, place, blocks):
    me, n, per = me_ref[0], me_ref[1], me_ref[2]
    source = lax.rem(me - place // per + n, n) * per + lax.rem(place, per)
    out = blocks[0]
    for m in range(1, len(blocks)):
        out = jnp.where(source == m, blocks[m], out)
    return out


def lanes(ref, rows=slice(None)):
    return [ref[rows, m * QB : (m + 1) * QB] for m in range(ref.shape[1] // QB)]


def fwd_kernel(me_ref, q_ref, k_ref, v_ref, cos_ref, sin_ref, drow_ref, dcol_ref, fq_ref, fk_ref,
               qo, ko, vo, pqo, pko, atto, ctxo, mo, deno):
    heads = fq_ref.shape[0]
    hd = k_ref.shape[0]
    length = k_ref.shape[1]
    for block in range(length // QB):
        cols = slice(block * QB, (block + 1) * QB)
        cos, sin = cos_ref[:, cols], sin_ref[:, cols]
        ko[:, cols] = turned(block_pick(me_ref, block, lanes(k_ref)), cos, sin).astype(BF)
        vo[:, cols] = block_pick(me_ref, block, lanes(v_ref)).astype(BF)
        for j in range(heads):
            rows = slice(j * hd, (j + 1) * hd)
            qo[rows, cols] = turned(block_pick(me_ref, block, lanes(q_ref, rows)), cos, sin).astype(BF)
    kt = ko[...]
    vt = vo[...]
    keys = jnp.transpose(kt.astype(F32)).astype(BF)
    pkt = features(nn(fk_ref[0], kt)).astype(BF)
    pko[...] = pkt
    pk = jnp.transpose(pkt.astype(F32)).astype(BF)
    for j in range(heads):
        qt = qo[j * hd : (j + 1) * hd, :]
        pqo[j * 2 * hd : (j + 1) * 2 * hd, :] = features(nn(fq_ref[j], qt)).astype(BF)
    for q0 in range(0, length, QB):
        n = q0 + QB
        w0 = max(q0 - WIN, 0)
        l1 = n - WIN
        qcat = side([qo[j * hd : (j + 1) * hd, q0:n] for j in range(heads)])
        pcat = side([pqo[j * 2 * hd : (j + 1) * 2 * hd, q0:n] for j in range(heads)])
        window, _ = masks(drow_ref, dcol_ref, q0, w0, n - w0, heads)
        _, linear = masks(drow_ref, dcol_ref, q0, 0, l1, heads)
        s = nn(keys[w0:n], qcat) * hd ** (-0.5)
        s = jnp.where(window > 0, s, -1e30)
        m = jnp.max(s, axis=0, keepdims=True)
        w = jnp.exp(s - m)
        kd = jnp.where(linear > 0, nn(pk[:l1], pcat) * jnp.exp(-m), 0.0)
        den = jnp.sum(w, axis=0, keepdims=True) + jnp.sum(kd, axis=0, keepdims=True)
        a = mixed_rows(w, kd, w0, l1, n).astype(BF)
        out = nn(vt[:, :n], a) / den
        for j in range(heads):
            cols = slice(j * QB, (j + 1) * QB)
            atto[j * hd : (j + 1) * hd, q0:n] = out[:, cols]
            mo[0, j : j + 1, q0:n] = m[:, cols]
            deno[0, j : j + 1, q0:n] = den[:, cols]
    for place in range(length // QB):
        ctxo[:, place * QB : (place + 1) * QB] = block_pick(me_ref, place, lanes(atto)).astype(BF)


def bwd_kernel(me_ref, q_ref, k_ref, v_ref, pq_ref, pk_ref, att_ref, m_ref, den_ref, g_ref,
               cos_ref, sin_ref, drow_ref, dcol_ref, fq_ref, fk_ref,
               dqo, dko, dvo, dfqo, dfko,
               dq_s, dpq_s, dk_s, dv_s, dpk_s):
    heads = fq_ref.shape[0]
    hd = k_ref.shape[0]
    length = k_ref.shape[1]
    cos, sin = cos_ref[...], sin_ref[...]
    kt = k_ref[...]
    pkt = pk_ref[...]
    keys = jnp.transpose(kt.astype(F32)).astype(BF)
    vals = jnp.transpose(v_ref[...].astype(F32)).astype(BF)
    pk = jnp.transpose(pkt.astype(F32)).astype(BF)

    def store(ref, rows, value):
        for place in range(length // QB):
            block = block_pick(me_ref, place, [value[:, p : p + QB] for p in range(0, length, QB)])
            ref[rows, place * QB : (place + 1) * QB] = block.astype(BF)

    dk_s[...] = jnp.zeros_like(dk_s)
    dv_s[...] = jnp.zeros_like(dv_s)
    dpk_s[...] = jnp.zeros_like(dpk_s)
    scale = hd ** (-0.5)
    for q0 in range(0, length, QB):
        n = q0 + QB
        w0 = max(q0 - WIN, 0)
        l1 = n - WIN
        qcat = side([q_ref[j * hd : (j + 1) * hd, q0:n] for j in range(heads)])
        pcat = side([pq_ref[j * 2 * hd : (j + 1) * 2 * hd, q0:n] for j in range(heads)])
        gcat = block_pick(
            me_ref, q0 // QB,
            [side([g_ref[j * hd : (j + 1) * hd, p : p + QB] for j in range(heads)]).astype(F32)
             for p in range(0, length, QB)],
        ).astype(BF)
        acat = side([att_ref[j * hd : (j + 1) * hd, q0:n] for j in range(heads)])
        m = side([m_ref[0, j : j + 1, q0:n] for j in range(heads)])
        rden = 1.0 / side([den_ref[0, j : j + 1, q0:n] for j in range(heads)])
        gf = gcat.astype(F32)
        c = jnp.sum(gf * acat, axis=0, keepdims=True)
        window, _ = masks(drow_ref, dcol_ref, q0, w0, n - w0, heads)
        _, linear = masks(drow_ref, dcol_ref, q0, 0, l1, heads)
        db = (nn(vals[:n], gcat) - c) * rden
        s = nn(keys[w0:n], qcat) * scale
        s = jnp.where(window > 0, s, -1e30)
        w = jnp.exp(s - m)
        d = jnp.exp(-m)
        kd = jnp.where(linear > 0, nn(pk[:l1], pcat) * d, 0.0)
        b = mixed_rows(w, kd, w0, l1, n)
        dv_s[0:n, :] += nt(b.astype(BF), (gf * rden).astype(BF))
        dm = -jnp.sum(b * db, axis=0, keepdims=True)
        top = jnp.where(s == m, 1.0, 0.0)
        ties = jnp.sum(top, axis=0, keepdims=True)
        ds = ((w * db[w0:] + top * (dm / ties)) * scale).astype(BF)
        dqw = tn(keys[w0:n], ds)
        dk_s[w0:n, :] += nt(ds, qcat)
        dker = jnp.where(linear > 0, db[:l1] * d, 0.0).astype(BF)
        dpq = tn(pk[:l1], dker)
        dpk_s[0:l1, :] += nt(dker, pcat)
        for j in range(heads):
            cols = slice(j * QB, (j + 1) * QB)
            dq_s[j * hd : (j + 1) * hd, q0:n] = dqw[:, cols]
            dpq_s[j * 2 * hd : (j + 1) * 2 * hd, q0:n] = dpq[:, cols]
    for j in range(heads):
        rows = slice(j * hd, (j + 1) * hd)
        wide = slice(j * 2 * hd, (j + 1) * 2 * hd)
        dz = features_back(pq_ref[wide, :].astype(F32), dpq_s[wide, :]).astype(BF)
        dfqo[j] = nt(q_ref[rows, :], dz)
        store(dqo, rows, turned(dq_s[rows, :] + nn(fq_ref[j], dz), cos, -sin))
    dz = features_back(pkt.astype(F32), jnp.transpose(dpk_s[...])).astype(BF)
    dfko[0] = nt(kt, dz)
    dk = jnp.transpose(dk_s[...]) + nn(fk_ref[0], dz)
    store(dko, slice(None), turned(dk, cos, -sin))
    store(dvo, slice(None), jnp.transpose(dv_s[...]))


def attn_specs(nq, nk, hd, length):
    heads = nq // nk
    whole = lambda shape: pl.BlockSpec(shape, lambda g: (0,) * len(shape))
    return dict(
        me=pl.BlockSpec(memory_space=pltpu.SMEM),
        q=pl.BlockSpec((heads * hd, length), lambda g: (g, 0)),
        k=pl.BlockSpec((hd, length), lambda g: (g, 0)),
        kin=pl.BlockSpec((hd, length), lambda g: (nq + g, 0)),
        vin=pl.BlockSpec((hd, length), lambda g: (nq + nk + g, 0)),
        pq=pl.BlockSpec((2 * heads * hd, length), lambda g: (g, 0)),
        pk=pl.BlockSpec((2 * hd, length), lambda g: (g, 0)),
        row=pl.BlockSpec((1, heads, length), lambda g: (g, 0, 0)),
        angle=whole((hd // 2, length)),
        drow=whole((1, length)),
        dcol=whole((length, QB)),
        fq2=pl.BlockSpec((heads, 2 * hd, hd), lambda g: (g, 0, 0)),
        fk2=pl.BlockSpec((1, 2 * hd, hd), lambda g: (g, 0, 0)),
        fq=pl.BlockSpec((heads, hd, hd), lambda g: (g, 0, 0)),
        fk=pl.BlockSpec((1, hd, hd), lambda g: (g, 0, 0)),
    )


def attn_fwd(me, proj, cos, sin, drow, dcol, fq2, fk2):
    nq, nk, hd = fq2.shape[0], fk2.shape[0], fq2.shape[2]
    length = proj.shape[1]
    heads = nq // nk
    sp = attn_specs(nq, nk, hd, length)
    sds = jax.ShapeDtypeStruct
    pairs = length * length * nq
    return pl.pallas_call(
        fwd_kernel,
        grid=(nk,),
        in_specs=[sp["me"], sp["q"], sp["kin"], sp["vin"], sp["angle"], sp["angle"], sp["drow"], sp["dcol"],
                  sp["fq2"], sp["fk2"]],
        out_specs=[sp["q"], sp["k"], sp["k"], sp["pq"], sp["pk"], sp["q"], sp["q"], sp["row"], sp["row"]],
        out_shape=[
            sds((nq * hd, length), BF), sds((nk * hd, length), BF), sds((nk * hd, length), BF),
            sds((2 * nq * hd, length), BF), sds((2 * nk * hd, length), BF),
            sds((nq * hd, length), F32), sds((nq * hd, length), BF),
            sds((nk, heads, length), F32), sds((nk, heads, length), F32),
        ],
        cost_estimate=pl.CostEstimate(flops=8 * pairs * hd, bytes_accessed=8 << 20, transcendentals=pairs),
        compiler_params=pltpu.CompilerParams(vmem_limit_bytes=48 << 20),
        name="attn_fwd",
    )(me, proj, proj, proj, cos, sin, drow, dcol, fq2, fk2)


def attn_bwd(me, saved, g, cos, sin, drow, dcol, fq, fk):
    qt, kt, vt, pq, pk, att, m, den = saved
    nq, nk, hd = fq.shape[0], fk.shape[0], fq.shape[2]
    length = qt.shape[1]
    heads = nq // nk
    sp = attn_specs(nq, nk, hd, length)
    sds = jax.ShapeDtypeStruct
    pairs = length * length * nq
    return pl.pallas_call(
        bwd_kernel,
        grid=(nk,),
        in_specs=[sp["me"], sp["q"], sp["k"], sp["k"], sp["pq"], sp["pk"], sp["q"], sp["row"], sp["row"], sp["q"],
                  sp["angle"], sp["angle"], sp["drow"], sp["dcol"], sp["fq"], sp["fk"]],
        out_specs=[sp["q"], sp["k"], sp["k"], sp["fq"], sp["fk"]],
        out_shape=[
            sds((nq * hd, length), BF), sds((nk * hd, length), BF), sds((nk * hd, length), BF),
            sds((nq, hd, hd), F32), sds((nk, hd, hd), F32),
        ],
        scratch_shapes=[
            pltpu.VMEM((heads * hd, length), F32),
            pltpu.VMEM((2 * heads * hd, length), F32),
            pltpu.VMEM((length, hd), F32),
            pltpu.VMEM((length, hd), F32),
            pltpu.VMEM((length, 2 * hd), F32),
        ],
        cost_estimate=pl.CostEstimate(flops=20 * pairs * hd, bytes_accessed=8 << 20, transcendentals=pairs),
        compiler_params=pltpu.CompilerParams(vmem_limit_bytes=48 << 20),
        name="attn_bwd",
    )(me, qt, kt, vt, pq, pk, att, m, den, g, cos, sin, drow, dcol, fq, fk)


def ffn_kernel(x_ref, g_ref, wg_ref, wu_ref, wd_ref, out_ref, back_ref, prod_ref, dgate_ref, dup_ref,
               out_acc, back_acc):
    step = pl.program_id(1)
    x = x_ref[...]
    gate = nn(x, wg_ref[...])
    up = nn(x, wu_ref[...])
    sg = jax.nn.sigmoid(gate)
    act = gate * sg
    prod = (act * up).astype(BF)
    prod_ref[...] = prod
    gp = nt(g_ref[...], wd_ref[...])
    dgate = (gp * up * (sg + act * (1.0 - sg))).astype(BF)
    dup = (gp * act).astype(BF)
    dgate_ref[...] = dgate
    dup_ref[...] = dup
    out = nn(prod, wd_ref[...])
    back = nt(dgate, wg_ref[...]) + nt(dup, wu_ref[...])

    @pl.when(step == 0)
    def _():
        out_acc[...] = out
        back_acc[...] = back

    @pl.when(step > 0)
    def _():
        out_acc[...] += out
        back_acc[...] += back

    @pl.when(step == pl.num_programs(1) - 1)
    def _():
        out_ref[...] = out_acc[...].astype(BF)
        back_ref[...] = back_acc[...].astype(BF)


def ffn_both(x, g, w_both, wd):
    length, width = x.shape
    ff = wd.shape[0]
    tm, tf = min(512, length), min(512, ff)
    rows = pl.BlockSpec((tm, width), lambda i, j: (i, 0))
    cols = pl.BlockSpec((width, tf), lambda i, j: (0, j))
    tile = pl.BlockSpec((tm, tf), lambda i, j: (i, j))
    more = pl.BlockSpec((width, tf), lambda i, j: (0, ff // tf + j))
    sds = jax.ShapeDtypeStruct
    return pl.pallas_call(
        ffn_kernel,
        grid=(length // tm, ff // tf),
        in_specs=[rows, rows, cols, more, pl.BlockSpec((tf, width), lambda i, j: (j, 0))],
        out_specs=[rows, rows, tile, tile, tile],
        out_shape=[sds((length, width), BF)] * 2 + [sds((length, ff), BF)] * 3,
        scratch_shapes=[pltpu.VMEM((tm, width), F32)] * 2,
        cost_estimate=pl.CostEstimate(
            flops=12 * length * width * ff, bytes_accessed=6 * width * ff, transcendentals=length * ff
        ),
        compiler_params=pltpu.CompilerParams(vmem_limit_bytes=56 << 20),
        name="ffn_both",
    )(x, g, w_both, w_both, wd)


def weight_grad(pairs, x_dim, y_dim, by_rows, side_index, others=None, add=None):
    x0, y0 = pairs[0]
    tokens, rows, cols = x0.shape[x_dim], x0.shape[1 - x_dim], y0.shape[1 - y_dim]
    groups = lax.axis_size("grp")
    half = groups // 2
    count = len(pairs)
    extra = 0 if add is None else 1

    def kernel(side_ref, *refs):
        out = refs[-1]

        def cut(ref, dim, size, which):
            place = slice(which * size, (which + 1) * size)
            return ref[:, place] if dim == 0 else ref[place, :]

        for which in range(2):

            @pl.when(side_ref[0] == which)
            def _(which=which):
                total = None
                for k in range(count):
                    x, y = refs[2 * k], refs[2 * k + 1]
                    x = cut(x, x_dim, tm, which) if by_rows else x[...]
                    y = y[...] if by_rows else cut(y, y_dim, tn, which)
                    part = lax.dot_general(x, y, (((x_dim,), (y_dim,)), ((), ())), preferred_element_type=F32)
                    total = part if total is None else total + part
                total = total.reshape(out.shape)
                if extra:
                    total = total + refs[2 * count][...].astype(F32)
                out[...] = total.astype(BF)

    def spec(dim, size, where):
        if dim == 0:
            return pl.BlockSpec((tokens, size), lambda i, j: (0, where(i, j)))
        return pl.BlockSpec((size, tokens), lambda i, j: (where(i, j), 0))

    if by_rows:
        shards = lax.axis_size("shard")
        part = rows // shards // groups
        tm, tn = half * part, cols
        grid = (shards, 1)
        xs = spec(x_dim, 2 * tm, lambda i, j: i)
        ys = spec(y_dim, tn, lambda i, j: j)
        shape = (half, shards, part, cols)
        block = pl.BlockSpec((half, 1, part, tn), lambda i, j: (0, i, 0, j))
    else:
        tm, tn = min(1024, rows), cols // groups
        grid = (rows // tm, half)
        xs = spec(x_dim, tm, lambda i, j: i)
        ys = spec(y_dim, 2 * tn, lambda i, j: j)
        shape = (half, rows, tn)
        block = pl.BlockSpec((1, tm, tn), lambda i, j: (j, i, 0))
    return pl.pallas_call(
        kernel,
        grid=grid,
        in_specs=[pl.BlockSpec(memory_space=pltpu.SMEM)] + [xs, ys] * count + [block] * extra,
        out_specs=block,
        out_shape=jax.ShapeDtypeStruct(shape, BF),
        cost_estimate=pl.CostEstimate(
            flops=count * tokens * rows * cols, bytes_accessed=rows * cols, transcendentals=0
        ),
        compiler_params=pltpu.CompilerParams(vmem_limit_bytes=48 << 20),
        name="weight_grad",
    )(side_index, *[a for pair in pairs for a in pair], *([add] if extra else []))


def tie(x, *others):
    return lax.optimization_barrier((x,) + others)[0] if others else x


def gather_small(x):
    SCOPE[0] = "small"
    n = lax.axis_size("shard")
    x = now(x)
    return [x] + [permute(x, "shard", [(k, (k + t) % n) for k in range(n)]) for t in range(1, n)]


SCOPE = ["start"]


def permute(x, axis, pairs):
    with jax.named_scope(SCOPE[0]):
        return lax.ppermute(x, axis, pairs)


class Clock:
    before, here = [], []


def now(x):
    return tie(x, *Clock.before)


def put(*values):
    Clock.here.extend(values)


def tick():
    Clock.before, Clock.here = Clock.here, []


class Gather:
    def __init__(self, x, name="gather"):
        self.name = name
        self.x, self.up, self.down = x, x, x
        self.ups, self.downs = [], []

    def step(self):
        n, t = lax.axis_size("shard"), len(self.ups) + 1
        if t >= n:
            return
        SCOPE[0] = self.name + str(t)
        self.up = permute(now(self.up), "shard", [(k, k + 1) for k in range(t - 1, n - 1)])
        self.down = permute(now(self.down), "shard", [(k, k - 1) for k in range(n - t, 0, -1)])
        self.ups.append(self.up)
        self.downs.append(self.down)
        put(self.up, self.down)

    def last(self):
        while len(self.ups) + 1 < lax.axis_size("shard"):
            self.step()

    def result(self):
        n, i = lax.axis_size("shard"), lax.axis_index("shard")
        blocks = [jnp.where(i >= t, self.ups[t - 1], self.downs[n - t - 1]) for t in range(1, n)]
        return jnp.concatenate([self.x] + blocks)


class Scatter:
    def __init__(self, x, name="scatter"):
        self.name = name
        n = lax.axis_size("shard")
        rows = x.shape[0] // n
        self.parts = [x[k * rows : (k + 1) * rows] for k in range(n)]
        self.got, self.t = {1: None, -1: None}, 0

    def step(self):
        n, t = len(self.parts), self.t + 1
        if t >= n:
            return
        SCOPE[0] = self.name + str(t)
        self.t = t
        for way in (1, -1):
            block = now(self.parts[t if way > 0 else n - t])
            if self.got[way] is not None:
                block = (block.astype(F32) + self.got[way].astype(F32)).astype(block.dtype)
            if way > 0:
                pairs = [(k, k + 1) for k in range(0, t)]
            else:
                pairs = [(k, k - 1) for k in range(n - 1, n - 1 - t, -1)]
            self.got[way] = permute(block, "shard", pairs)
            put(self.got[way])

    def last(self):
        while self.t + 1 < len(self.parts):
            self.step()

    def result(self):
        total = self.parts[0].astype(F32)
        for way in (1, -1):
            if self.got[way] is not None:
                total = total + self.got[way].astype(F32)
        return total


def gather_direct(x, name):
    SCOPE[0] = name
    n = lax.axis_size("shard")
    x = now(x)
    got = [permute(x, "shard", [(k, (k + t) % n) for k in range(n)]) for t in range(1, n)]
    put(*got)
    return jnp.concatenate([x] + got)


def scatter_direct(x, name):
    SCOPE[0] = name
    n = lax.axis_size("shard")
    rows = x.shape[0] // n
    x = now(x)
    got = [
        permute(x[t * rows : (t + 1) * rows], "shard", [(k, (k - t) % n) for k in range(n)]) for t in range(1, n)
    ]
    put(*got)
    return functools.reduce(lambda a, c: a + c.astype(F32), got, x[:rows].astype(F32))


def in_order(blocks):
    n, i = lax.axis_size("shard"), lax.axis_index("shard")
    return [pick(i, [blocks[(m - j) % n] for m in range(n)]) for j in range(n)]


def pick(i, cases):
    out = cases[0]
    for m in range(1, len(cases)):
        out = jnp.where(i == m, cases[m], out)
    return out


def swap_z(parts, name="swap"):
    n, i = lax.axis_size("shard"), lax.axis_index("shard")
    SCOPE[0] = name
    parts = now(parts)
    out = [lax.dynamic_index_in_dim(parts, i, 0, False)]
    for t in range(1, n):
        block = lax.dynamic_index_in_dim(parts, (i + t) % n, 0, False)
        out.append(permute(block, "shard", [(k, (k + t) % n) for k in range(n)]))
    put(*out[1:])
    return out


def scatter_small(p):
    return functools.reduce(lambda a, c: a + c, [part.astype(F32) for part in swap_z(p)])


def swapped_rows(name, pieces, hold):
    n, i = lax.axis_size("shard"), lax.axis_index("shard")
    size, g = lax.axis_size("grp"), lax.axis_index("grp")
    rows = pieces[0].shape[0] // size
    SCOPE[0] = name

    def part(d):
        cut = []
        for w in pieces:
            cols = w.shape[1] // n
            cut.append(lax.dynamic_slice(w, (g * rows, d * cols), (rows, cols)))
        return jnp.concatenate(cut, axis=1) if len(cut) > 1 else cut[0]

    blocks = [part(i)]
    for t in range(1, n):
        block = now(part((i + t) % n))
        blocks.append(permute(block, "shard", [(k, (k + t) % n) for k in range(n)]))
    if hold:
        put(*blocks[1:])
    return jnp.stack(in_order(blocks))


def all_rows(part):
    n, rows, cols = part.shape
    return lax.all_gather(part, "grp", axis=1).reshape(n * lax.axis_size("grp") * rows, cols)


class Halves:
    def __init__(self, name, pairs, x_dim, y_dim, by_rows):
        self.name = name
        self.args = (pairs, x_dim, y_dim, by_rows)

    def half(self, which, **more):
        (x, y), *rest = self.args[0]
        which = jnp.stack([which]).astype(jnp.int32)
        return weight_grad([(now(x), y)] + rest, *self.args[1:], which, **more)

    def send(self):
        self.sent = self.half(1 - lax.axis_index("grp") % 2)
        put(self.sent)

    def core(self):
        SCOPE[0] = self.name + "core"
        size = lax.axis_size("grp")
        self.come = permute(now(self.sent), "grp", [(k, k ^ 1) for k in range(size)])
        put(self.come)

    def keep(self):
        self.value = self.half(lax.axis_index("grp") % 2, add=self.come)
        put(self.value)

    def finish(self):
        size = lax.axis_size("grp")
        flat = self.value.reshape((-1,) + self.value.shape[2:])
        alike = [[k for k in range(size) if k % 2 == c] for c in range(2)]
        return lax.psum_scatter(flat, "grp", scatter_dimension=0, axis_index_groups=alike, tiled=True)


def column_grads(part, widths):
    n, size = lax.axis_size("shard"), lax.axis_size("grp")
    rows = part.shape[1]
    outs, start = [], 0
    for group in widths:
        cols = []
        for width in group:
            cols.append(jnp.swapaxes(part[:, :, start : start + width], 0, 1).reshape(rows, n * width))
            start += width
        whole = jnp.concatenate(cols, axis=1) if len(cols) > 1 else cols[0]
        moved = lax.all_to_all(whole, "grp", 1, 0, tiled=True)
        moved = jnp.swapaxes(moved.reshape(size // 2, 2, rows, -1), 0, 1).reshape(size * rows, -1)
        outs.append(moved.astype(F32))
    return outs


def group_sum(x):
    SCOPE[0] = "groupsum"
    size = lax.axis_size("grp")
    step = 1
    while step < size:
        got = lax.ppermute(x, "grp", [(k, k ^ step) for k in range(size)])
        x = (x.astype(F32) + got.astype(F32)).astype(BF)
        step *= 2
    return x.astype(F32)


def norm_scale(h):
    return lax.rsqrt(jnp.mean(h * h, axis=-1, keepdims=True) + EPS)


def norm_back(h, gain, gn):
    r = norm_scale(h)
    g = gn * gain
    grad = r * g - h * (r * r * r) * jnp.mean(g * h, axis=-1, keepdims=True)
    return grad, jnp.sum(gn * h * r, axis=0)


def body(
    tokens,
    cotangent,
    sequence_lengths,
    attention_norm_gain,
    query_matrix,
    key_value_matrix,
    output_matrix,
    adapter_down_maps,
    adapter_up_query,
    adapter_up_key_value,
    adapter_down_output,
    adapter_up_output,
    query_feature_matrices,
    key_feature_matrices,
    feedforward_norm_gain,
    gate_matrix,
    up_matrix,
    down_matrix,
):
    n, shard, size = lax.axis_size("shard"), lax.axis_index("shard"), lax.axis_size("grp")
    batches, _, rows, width = tokens.shape
    length = n * rows
    share = width // n
    nq, hd = query_feature_matrices.shape[:2]
    nk = key_feature_matrices.shape[0]
    rank = adapter_up_query.shape[0]
    qw, kw = nq * hd, nk * hd
    ffq = down_matrix.shape[0]

    small = jnp.concatenate(
        [
            attention_norm_gain[None],
            feedforward_norm_gain[None],
            adapter_up_output,
            adapter_down_maps.T,
        ],
        axis=0,
    )
    half_kv = key_value_matrix.shape[1] // 2
    ends = jnp.cumsum(sequence_lengths[:, 0], axis=1)
    last = sequence_lengths.shape[2] - 2
    own = shard * rows + jnp.arange(rows, dtype=jnp.int32)
    gm_own = [jnp.where((own < ends[b, last])[:, None], cotangent[b, 0], 0) for b in range(batches)]
    me = jnp.stack([shard, jnp.int32(n), jnp.int32(rows // QB)]).astype(jnp.int32)
    Clock.before, Clock.here = [], []
    tok = [Gather(tokens[b, 0], f"tok{b}x") for b in range(batches)]
    cot0 = Gather(gm_own[0], "cot0x")
    s_qkv = swapped_rows("sqkv", [query_matrix, key_value_matrix[:, :half_kv], key_value_matrix[:, half_kv:]], True)
    tok[0].step()
    tick()
    w_qkv = all_rows(s_qkv)
    small_full = jnp.concatenate(in_order(gather_small(small)), axis=1)
    gain_attn = small_full[0].astype(F32)
    gain_ffn = small_full[1].astype(F32)
    up_output = small_full[2 : 2 + rank]
    down_maps_t = small_full[2 + rank :]
    tok[0].step()
    tick()
    tok[0].last()
    tick()
    tok[1].step()
    s_both = swapped_rows("sgu", [gate_matrix, up_matrix], False)
    pad = jnp.zeros((qw, -rank % 128), BF)
    out_wide = jnp.concatenate([output_matrix, adapter_down_output, pad], axis=1)
    zero = jnp.zeros
    u_all = jnp.concatenate(
        [
            jnp.concatenate([adapter_up_query, zero((rank, 2 * kw), BF)], axis=1),
            jnp.concatenate([zero((rank, qw), BF), adapter_up_key_value[0], zero((rank, kw), BF)], axis=1),
            jnp.concatenate([zero((rank, qw + kw), BF), adapter_up_key_value[1]], axis=1),
        ],
        axis=0,
    )

    begins = ends - sequence_lengths[:, 0]
    where = jnp.arange(length, dtype=jnp.int32)
    docs = jnp.sum((where[None, :, None] >= ends[:, None, :]).astype(jnp.int32), axis=2)
    relative = where[None] - jnp.max(
        jnp.where(where[None, :, None] >= begins[:, None, :], begins[:, None, :], 0), axis=2
    )
    freq = ROPE_BASE ** (-jnp.arange(hd // 2, dtype=F32) / (hd // 2))
    angles = freq[None, :, None] * relative.astype(F32)[:, None, :]
    cos_all, sin_all = jnp.cos(angles), jnp.sin(angles)

    def doubled(f):
        return jnp.swapaxes(jnp.concatenate([f, -f], axis=2), 1, 2)

    fq2, fk2 = doubled(query_feature_matrices), doubled(key_feature_matrices)

    def attention(b):
        x = now(tok[b].result()).astype(F32)
        normed = (x * norm_scale(x) * gain_attn).astype(BF)
        mid = nt(normed, down_maps_t).astype(BF)
        proj = lax.dot_general(w_qkv, normed, (((0,), (1,)), ((), ())), preferred_element_type=F32)
        proj = proj + lax.dot_general(u_all, mid, (((0,), (1,)), ((), ())), preferred_element_type=F32)
        place = (
            cos_all[b],
            sin_all[b],
            docs[b][None],
            jnp.broadcast_to(docs[b][:, None], (length, QB)),
        )
        qt, kt, vt, pq, pk, att, ctx, m, den = attn_fwd(me, proj, *place, fq2, fk2)
        branch = tn(ctx, out_wide).astype(BF)
        put(branch)
        return dict(normed=normed, mid=mid, saved=(qt, kt, vt, pq, pk, att, m, den), ctx=ctx, place=place,
                    branch=Scatter(branch, f"br{b}x"))

    def after_attention(b):
        k = keep[b]
        branch = k["branch"].result()
        lora_own = branch[:, width : width + rank].astype(BF)
        x_own = tokens[b, 0].astype(F32)
        hidden = x_own + branch[:, :width] + nn(lora_own, up_output)
        normed_own = (hidden * norm_scale(hidden) * gain_ffn).astype(BF)
        k.update(lora=lora_own, x=x_own, hidden=hidden, send=Gather(normed_own, f"nf{b}x"))

    def ffn(b, cot):
        k = keep[b]
        nf = k["send"].result()
        out, back, product, dgate, dup = ffn_both(now(nf), cot, w_both, down_matrix)
        put(dup)
        k.update(nf=nf, gm=cot, out=out, back=back, product=product, dgate=dgate, dup=dup)

    def after_ffn(b, gnf):
        k = keep[b]
        back, ffn_gain = norm_back(k["hidden"], gain_ffn, gnf)
        grad_hidden = gm_own[b].astype(F32) + back
        gb_own = grad_hidden.astype(BF)
        k.update(grad_hidden=grad_hidden, gb_own=gb_own, send=Gather(gb_own, f"gb{b}x"), ffn_gain=ffn_gain)

    def attention_back(b):
        k = keep[b]
        gb = now(k["send"].result())
        glo = nt(gb, up_output)
        gctx = nt(output_matrix, gb) + nt(adapter_down_output.astype(F32), glo)
        dq, dk, dv, dfq, dfk = attn_bwd(
            me, k["saved"], gctx.astype(BF), *k["place"], query_feature_matrices, key_feature_matrices
        )
        dqkv = jnp.concatenate([dq, dk, dv], axis=0)
        glm = tn(dqkv, u_all.T)
        gn = lax.dot_general(dqkv, w_qkv, (((0,), (1,)), ((), ())), preferred_element_type=F32)
        gn = (gn + nn(glm, down_maps_t.astype(F32))).astype(BF)
        put(gn)
        both = jnp.concatenate([gn, k["out"]], axis=1)
        k.update(gb=gb, glo=glo, dqkv=dqkv, glm=glm, dfq=dfq, dfk=dfk, gn=Scatter(both, f"gn{b}x"))

    def pairs(one, two):
        return [(k[one], k[two]) for k in keep]

    tick()
    keep = [attention(0)]
    tok[1].step()
    tick()
    w_both = all_rows(now(s_both))
    keep[0]["branch"].step()
    tok[1].last()
    keep[0]["branch"].step()
    tick()
    keep.append(attention(1))
    keep[0]["branch"].last()
    tick()
    after_attention(0)
    keep[0]["send"].step()
    tick()
    keep[0]["send"].step()
    keep[1]["branch"].step()
    tick()
    keep[0]["send"].last()
    keep[1]["branch"].step()
    tick()
    keep[1]["branch"].last()
    cot0.step()
    tick()
    after_attention(1)
    keep[1]["send"].step()
    cot0.step()
    tick()
    keep[1]["send"].step()
    cot0.last()
    tick()
    keep[1]["send"].last()
    tick()
    ffn(0, cot0.result())
    cot1 = gather_direct(gm_own[1], "cot1x")
    tick()
    ffn(1, cot1)
    gnf0 = scatter_direct(keep[0]["back"], "gnf0x")
    tick()
    w_g = Halves("Wg", pairs("nf", "dgate"), 0, 0, True)
    w_u = Halves("Wu", pairs("nf", "dup"), 0, 0, True)
    w_d = Halves("Wd", pairs("product", "gm"), 0, 0, False)
    gnf1 = Scatter(keep[1]["back"], "gnf1x")
    after_ffn(0, gnf0)
    keep[0]["send"].step()
    w_g.send()
    w_u.send()
    tick()
    keep[0]["send"].step()
    gnf1.step()
    w_g.core()
    w_d.send()
    tick()
    keep[0]["send"].last()
    gnf1.step()
    w_u.core()
    w_g.keep()
    r_g = w_g.finish()
    tick()
    gnf1.last()
    w_d.core()
    attention_back(0)
    w_u.keep()
    r_u = w_u.finish()
    tick()
    after_ffn(1, gnf1.result())
    keep[1]["send"].step()
    w_d.keep()
    r_d = w_d.finish()
    tick()
    keep[1]["send"].step()
    keep[0]["gn"].step()
    tick()
    keep[1]["send"].last()
    keep[0]["gn"].step()
    put(r_g)
    tick()
    attention_back(1)
    keep[0]["gn"].last()
    t_g = swap_z(r_g.reshape(n, -1, ffq), "swapg")
    tick()
    w_q = Halves("Wq", pairs("normed", "dqkv"), 0, 1, True)
    w_o = Halves("Wo", pairs("ctx", "gb"), 1, 0, False)
    w_q.send()
    w_o.send()
    keep[1]["gn"].step()
    put(r_u)
    tick()
    keep[1]["gn"].step()
    w_q.core()
    w_o.core()
    put(r_d)
    tick()
    keep[1]["gn"].last()
    t_u = swap_z(r_u.reshape(n, -1, ffq), "swapu")
    w_q.keep()
    r_q = w_q.finish()
    w_o.keep()
    r_o = w_o.finish()
    (grad_gate,) = column_grads(jnp.stack(in_order(t_g)), [[ffq]])
    tick()
    (grad_up,) = column_grads(jnp.stack(in_order(t_u)), [[ffq]])
    t_q = jnp.stack(in_order(swap_z(r_q.reshape(n, -1, qw + 2 * kw), "swapq")))
    grad_query, grad_kv = column_grads(t_q, [[qw], [kw, kw]])
    grad_down = r_d.astype(F32)
    grad_output = r_o.astype(F32)
    for k in keep:
        k["up_out"] = tn(k["lora"], k["gb_own"])
    output = []
    token_grads = []
    for k in keep:
        summed = k["gn"].result()
        output.append((k["hidden"] + summed[:, width:]).astype(BF))
        back, attn_gain = norm_back(k["x"], gain_attn, summed[:, :width])
        token_grads.append((k["grad_hidden"] + back).astype(BF))
        k.update(attn_gain=attn_gain)

    def both(name, axis=0):
        return jnp.concatenate([k[name] for k in keep], axis=axis)

    def added(name):
        return functools.reduce(lambda a, c: a + c, [k[name] for k in keep])

    normed = both("normed")
    ctx = both("ctx", 1)
    dqkv = both("dqkv", 1)
    glm = both("glm")
    down_maps_grad = tn(normed.astype(F32), glm)
    ups = lax.dot_general(both("mid"), dqkv, (((0,), (1,)), ((), ())), preferred_element_type=F32)
    down_out_grad = nn(ctx.astype(F32), both("glo"))
    spread = [
        added("attn_gain").reshape(n, share),
        added("ffn_gain").reshape(n, share),
        down_maps_grad.reshape(n, share * 3 * rank),
        jnp.swapaxes(added("up_out").reshape(rank, n, share), 0, 1).reshape(n, rank * share),
    ]
    lined = scatter_small(jnp.concatenate(spread, axis=1).astype(BF))
    local = [
        ups[:rank, :qw].reshape(-1),
        ups[rank : 2 * rank, qw : qw + kw].reshape(-1),
        ups[2 * rank :, qw + kw :].reshape(-1),
        down_out_grad.reshape(-1),
        added("dfq").reshape(-1),
        added("dfk").reshape(-1),
    ]
    flat = group_sum(jnp.concatenate([lined] + local).astype(BF))
    shapes = [
        (share,),
        (share,),
        (share, 3 * rank),
        (rank, share),
        (rank, qw),
        (rank, kw),
        (rank, kw),
        (qw, rank),
        (nq, hd, hd),
        (nk, hd, hd),
    ]
    got, start = [], 0
    for shape in shapes:
        count = 1
        for extent in shape:
            count *= extent
        got.append(flat[start : start + count].reshape(shape))
        start += count
    g_attn, g_ffn, g_down_maps, g_up_out, g_up_q, g_up_k, g_up_v, g_down_out, g_fq, g_fk = got
    return (
        jnp.stack(output)[:, None],
        jnp.stack(token_grads)[:, None],
        g_attn,
        grad_query,
        grad_kv,
        grad_output,
        g_down_maps,
        g_up_q,
        jnp.stack([g_up_k, g_up_v]),
        g_down_out,
        g_up_out,
        g_fq,
        g_fk,
        g_ffn,
        grad_gate,
        grad_up,
        grad_down,
    )


def solution(mesh):
    placed = (
        P(None, "grp", "shard", None),
        P(None, "grp", "shard", None),
        P(None, "grp", None),
        P("shard"),
        P("shard", None),
        P("shard", None),
        P("shard", None),
        P("shard", None),
        P(None, "shard"),
        P(None, None, "shard"),
        P("shard", None),
        P(None, "shard"),
        P("shard", None, None),
        P("shard", None, None),
        P("shard"),
        P("shard", None),
        P("shard", None),
        P("shard", None),
    )
    return jax.shard_map(
        body,
        mesh=mesh,
        in_specs=placed,
        out_specs=(
            P(None, "grp", "shard", None),
            P(None, "grp", "shard", None),
            P("shard"),
            P("shard", "grp"),
            P("shard", "grp"),
            P("shard", "grp"),
            P("shard", None),
            P(None, "shard"),
            P(None, None, "shard"),
            P("shard", None),
            P(None, "shard"),
            P("shard", None, None),
            P("shard", None, None),
            P("shard"),
            P("shard", "grp"),
            P("shard", "grp"),
            P("shard", "grp"),
        ),
        check_vma=False,
    )
```

profile of v0, /device:TPU:0, one launch (start us, length us, event | category | flops | bytes accessed | tf_op | source)
XLA Modules:
  0.0 930.5 jit_solution(3152647096452876422)
XLA Ops:
  61.1 10.0 %collective-permute-done.7 = bf16[128,2048]{1,0:T(8,128)(2,1)S(1)} collective-permute-done((bf16[128,2048]{1,0:T(8,128)(2,1)}, bf16[128,2048]{1,0:T(8,128)(2,1)S(1)}, u32[]{:S(2)}, u32[]{:S(2)}) %collective-permute-start.7) | collective-permute-done | bytes 524320 | tf_op jit(solution)/shard_map/tok0x3/ppermute | solution.py:435
  96.0 8.6 collective-permute-done.48
  104.5 27.6 %collective-permute-done.49 = bf16[64,4096]{1,0:T(8,128)(2,1)S(1)} collective-permute-done((bf16[64,4096]{1,0:T(8,128)(2,1)S(1)}, bf16[64,4096]{1,0:T(8,128)(2,1)S(1)}, u32[]{:S(2)}, u32[]{:S(2)}) %collective-permute-start.49) | collective-permute-done | bytes 524320 | tf_op jit(solution)/shard_map/sgu/ppermute | solution.py:435
  158.5 8.8 collective-permute-done.16
  174.1 9.8 %collective-permute-done.20 = bf16[128,2176]{1,0:T(8,128)(2,1)S(1)} collective-permute-done((bf16[128,2176]{1,0:T(8,128)(2,1)S(1)}, bf16[128,2176]{1,0:T(8,128)(2,1)S(1)}, u32[]{:S(2)}, u32[]{:S(2)}) %collective-permute-start.20) | collective-permute-done | bytes 557088 | tf_op jit(solution)/shard_map/br0x2/ppermute | solution.py:435
  214.5 8.5 collective-permute-done.24
  231.1 13.6 %collective-permute-done.26 = bf16[128,2048]{1,0:T(8,128)(2,1)S(1)} collective-permute-done((bf16[128,2048]{1,0:T(8,128)(2,1)S(1)}, bf16[128,2048]{1,0:T(8,128)(2,1)S(1)}, u32[]{:S(2)}, u32[]{:S(2)}) %collective-permute-start.26) | collective-permute-done | bytes 524320 | tf_op jit(solution)/shard_map/nf0x2/ppermute | solution.py:435
  251.5 11.5 %collective-permute-done.30 = bf16[128,2048]{1,0:T(8,128)(2,1)S(1)} collective-permute-done((bf16[128,2048]{1,0:T(8,128)(2,1)S(1)}, bf16[128,2048]{1,0:T(8,128)(2,1)S(1)}, u32[]{:S(2)}, u32[]{:S(2)}) %collective-permute-start.30) | collective-permute-done | bytes 524320 | tf_op jit(solution)/shard_map/nf0x3/ppermute | solution.py:435
  285.3 8.4 collective-permute-done.37
  302.2 21.5 %collective-permute-done.41 = bf16[128,2048]{1,0:T(8,128)(2,1)S(1)} collective-permute-done((bf16[128,2048]{1,0:T(8,128)(2,1)S(1)}, bf16[128,2048]{1,0:T(8,128)(2,1)S(1)}, u32[]{:S(2)}, u32[]{:S(2)}) %collective-permute-start.41) | collective-permute-done | bytes 524320 | tf_op jit(solution)/shard_map/cot0x2/ppermute | solution.py:435
  336.6 12.8 %collective-permute-done.43 = bf16[128,2048]{1,0:T(8,128)(2,1)S(1)} collective-permute-done((bf16[128,2048]{1,0:T(8,128)(2,1)S(1)}, bf16[128,2048]{1,0:T(8,128)(2,1)S(1)}, u32[]{:S(2)}, u32[]{:S(2)}) %collective-permute-start.43) | collective-permute-done | bytes 524320 | tf_op jit(solution)/shard_map/nf1x2/ppermute | solution.py:435
  353.3 11.5 %collective-permute-done.47 = bf16[128,2048]{1,0:T(8,128)(2,1)S(1)} collective-permute-done((bf16[128,2048]{1,0:T(8,128)(2,1)S(1)}, bf16[128,2048]{1,0:T(8,128)(2,1)S(1)}, u32[]{:S(2)}, u32[]{:S(2)}) %collective-permute-start.47) | collective-permute-done | bytes 524320 | tf_op jit(solution)/shard_map/nf1x3/ppermute | solution.py:435
  380.3 10.2 %collective-permute-done.52 = bf16[128,2048]{1,0:T(8,128)(2,1)S(1)} collective-permute-done((bf16[128,2048]{1,0:T(8,128)(2,1)S(1)}, bf16[128,2048]{1,0:T(8,128)(2,1)S(1)}, u32[]{:S(2)}, u32[]{:S(2)}) %collective-permute-start.52) | collective-permute-done | bytes 524320 | tf_op jit(solution)/shard_map/cot1x/ppermute | solution.py:435
  392.2 38.5 %ffn_both.2 = (bf16[512,2048]{1,0:T(8,128)(2,1)}, bf16[512,2048]{1,0:T(8,128)(2,1)}, bf16[512,2048]{1,0:T(8,128)(2,1)}, bf16[512,2048]{1,0:T(8,128)(2,1)}, bf16[512,2048]{1,0:T(8,128)(2,1)}) custom-call(bf16[512,2048]{1,0:T(8,128)(2,1)} %pad_maximum_fusion.2.x_ref.refs_0_, bf16[512,2048]{1,0:T(8,128)(2,1)} %pad_maximum_fusion.3.g_ref.refs_1_, ...), custom_call_target="tpu_custom_call" | custom-call | flops 25769803776 | bytes 25165824 | tf_op jit(solution)/shard_map/ffn_both/pallas_call | solution.py:338
  440.8 38.8 %ffn_both.3 = (bf16[512,2048]{1,0:T(8,128)(2,1)}, bf16[512,2048]{1,0:T(8,128)(2,1)}, bf16[512,2048]{1,0:T(8,128)(2,1)}, bf16[512,2048]{1,0:T(8,128)(2,1)}, bf16[512,2048]{1,0:T(8,128)(2,1)}) custom-call(bf16[512,2048]{1,0:T(8,128)(2,1)} %pad_maximum_fusion.5.x_ref.refs_2_, bf16[512,2048]{1,0:T(8,128)(2,1)} %constant_dynamic-update-slice_fusion.g_ref.refs_3_, ...), custom_call_target="tpu_custom_call" | custom-call | flops 25769803776 | bytes 25165824 | tf_op jit(solution)/shard_map/ffn_both/pallas_call | solution.py:338
  519.3 10.4 %weight_grad.12 = bf16[4,2048,256]{2,1,0:T(8,128)(2,1)} custom-call(s32[1]{0:T(128)} %bitcast.34.side_ref, bf16[512,2048]{1,0:T(8,128)(2,1)S(1)} %copy-done.11, bf16[512,2048]{1,0:T(8,128)(2,1)S(1)} %copy-done.6, bf16[512,2048]{1,0:T(8,128)(2,1)} %get-tuple-element.215.refs_2_, bf16[512,2048]{1,0:T(8,128)(2,1)} %constant_dynamic-update-slice_fusion.g_ref.refs_3_), custom_call_target="tpu_custom_call" | custom-call | flops 4294967296 | bytes 4194304 | tf_op jit(solution)/shard_map/weight_grad/pallas_call | solution.py:405
  534.6 8.9 weight_grad.13
  551.0 8.9 collective-permute-done.66
  569.5 8.9 weight_grad.14
  621.6 11.3 %weight_grad.15 = bf16[4,2048,256]{2,1,0:T(8,128)(2,1)} custom-call(s32[1]{0:T(128)} %bitcast.35.side_ref, bf16[512,2048]{1,0:T(8,128)(2,1)S(1)} %copy-done.12, bf16[512,2048]{1,0:T(8,128)(2,1)S(1)} %copy-done.7, bf16[512,2048]{1,0:T(8,128)(2,1)} %get-tuple-element.215.refs_2_, bf16[512,2048]{1,0:T(8,128)(2,1)} %constant_dynamic-update-slice_fusion.g_ref.refs_3_, ...), custom_call_target="tpu_custom_call" | custom-call | flops 4294967296 | bytes 4194304 | tf_op jit(solution)/shard_map/weight_grad/pallas_call | solution.py:405
  678.3 14.4 %collective-permute-done.80 = bf16[128,4096]{1,0:T(8,128)(2,1)} collective-permute-done((bf16[128,4096]{1,0:T(8,128)(2,1)}, bf16[128,4096]{1,0:T(8,128)(2,1)}, u32[]{:S(2)}, u32[]{:S(2)}) %collective-permute-start.80) | collective-permute-done | bytes 1048608 | tf_op jit(solution)/shard_map/gn0x2/ppermute | solution.py:435
  727.4 8.7 collective-permute-done.82
  737.8 9.3 %collective-permute-start.87 = (bf16[128,4096]{1,0:T(8,128)(2,1)}, bf16[128,4096]{1,0:T(8,128)(2,1)}, u32[]{:S(2)}, u32[]{:S(2)}) collective-permute-start(bf16[128,4096]{1,0:T(8,128)(2,1)} %get-tuple-element.263), channel_id=1, source_target_pairs={{0,1},{4,5},{8,9},{12,13},{16,17},{20,21},{24,25},{28,29}} | collective-permute-start | bytes 3145736 | tf_op jit(solution)/shard_map/gn1x1/ppermute | solution.py:435
  790.6 10.1 %collective-permute-done.89 = bf16[128,4096]{1,0:T(8,128)(2,1)} collective-permute-done((bf16[128,4096]{1,0:T(8,128)(2,1)}, bf16[128,4096]{1,0:T(8,128)(2,1)}, u32[]{:S(2)}, u32[]{:S(2)}) %collective-permute-start.89) | collective-permute-done | bytes 1048608 | tf_op jit(solution)/shard_map/gn1x2/ppermute | solution.py:435
  (887 shorter events, 581.1 us)
Async XLA Ops:
  7.2 127.2 %all-gather.5.cloned.1.call-start = ((), (), s32[]{:S(2)}) async-start(), calls=%async_computation.14 | async-start | bytes 3538944 | tf_op jit(solution)/shard_map/all_gather | solution.py:591
  9.6 32.1 %collective-permute-start.3 = (bf16[128,2048]{1,0:T(8,128)(2,1)}, bf16[128,2048]{1,0:T(8,128)(2,1)}, u32[]{:S(2)}, u32[]{:S(2)}) collective-permute-start(bf16[128,2048]{1,0:T(8,128)(2,1)} %get-tuple-element.439), channel_id=1, source_target_pairs={{0,1},{1,2},{2,3},{4,5},{5,6},{6,7},{8,9},{9,10},{10,11},{12,13},{... | collective-permute-start | bytes 1572872 | tf_op jit(solution)/shard_map/tok0x1/ppermute | solution.py:435
  41.6 350.6 %all-gather.7.cloned.1.call-start = ((), (), s32[]{:S(2)}) async-start(), calls=%async_computation.15 | async-start | bytes 18874368 | tf_op jit(solution)/shard_map/all_gather | solution.py:591
  78.0 54.1 %collective-permute-start.49 = (bf16[64,4096]{1,0:T(8,128)(2,1)S(1)}, bf16[64,4096]{1,0:T(8,128)(2,1)S(1)}, u32[]{:S(2)}, u32[]{:S(2)}) collective-permute-start(bf16[64,4096]{1,0:T(8,128)(2,1)S(1)} %copy-done.130), channel_id=1, source_target_pairs={{0,2},{1,3},{2,0},{3,1},{4,6},{5,7},{6,4},{7,5},{8,10},{9,11},{10,... | collective-permute-start | bytes 1572872 | tf_op jit(solution)/shard_map/sgu/ppermute | solution.py:435
  79.3 52.9 %collective-permute-start.50 = (bf16[64,4096]{1,0:T(8,128)(2,1)S(1)}, bf16[64,4096]{1,0:T(8,128)(2,1)S(1)}, u32[]{:S(2)}, u32[]{:S(2)}) collective-permute-start(bf16[64,4096]{1,0:T(8,128)(2,1)S(1)} %copy-done.129), channel_id=1, source_target_pairs={{0,1},{1,2},{2,3},{3,0},{4,5},{5,6},{6,7},{7,4},{8,9},{9,10},{10,1... | collective-permute-start | bytes 1572872 | tf_op jit(solution)/shard_map/sgu/ppermute | solution.py:435
  89.3 57.0 %collective-permute-start.14 = (bf16[128,2048]{1,0:T(8,128)(2,1)}, bf16[128,2048]{1,0:T(8,128)(2,1)}, u32[]{:S(2)}, u32[]{:S(2)}) collective-permute-start(bf16[128,2048]{1,0:T(8,128)(2,1)} %collective-permute-done.9), channel_id=1, source_target_pairs={{1,2},{2,3},{5,6},{6,7},{9,10},{10,11},{13,14},{14,15},{17,18},{18... | collective-permute-start | bytes 1572872 | tf_op jit(solution)/shard_map/tok1x2/ppermute | solution.py:435
  90.7 55.6 %collective-permute-start.15 = (bf16[128,2048]{1,0:T(8,128)(2,1)}, bf16[128,2048]{1,0:T(8,128)(2,1)}, u32[]{:S(2)}, u32[]{:S(2)}) collective-permute-start(bf16[128,2048]{1,0:T(8,128)(2,1)} %collective-permute-done.10), channel_id=1, source_target_pairs={{2,1},{1,0},{6,5},{5,4},{10,9},{9,8},{14,13},{13,12},{18,17},{17,1... | collective-permute-start | bytes 1572872 | tf_op jit(solution)/shard_map/tok1x2/ppermute | solution.py:435
  146.4 531.9 %reduce-scatter.6.cloned.1.call-start = ((), (), s32[]{:S(2)}) async-start(), calls=%async_computation.9 | async-start | bytes 5242880 | tf_op jit(solution)/shard_map/reduce_scatter | solution.py:622
  433.3 46.3 %collective-permute-start.54 = (bf16[128,2048]{1,0:T(8,128)(2,1)}, bf16[128,2048]{1,0:T(8,128)(2,1)S(1)}, u32[]{:S(2)}, u32[]{:S(2)}) collective-permute-start(bf16[128,2048]{1,0:T(8,128)(2,1)} %get-tuple-element.404), channel_id=1, source_target_pairs={{0,3},{1,0},{2,1},{3,2},{4,7},{5,4},{6,5},{7,6},{8,11},{9,8},{10,9... | collective-permute-start | bytes 1572872 | tf_op jit(solution)/shard_map/gnf0x/ppermute | solution.py:435
  439.8 39.7 %collective-permute-start.55 = (bf16[128,2048]{1,0:T(8,128)(2,1)}, bf16[128,2048]{1,0:T(8,128)(2,1)S(1)}, u32[]{:S(2)}, u32[]{:S(2)}) collective-permute-start(bf16[128,2048]{1,0:T(8,128)(2,1)} %get-tuple-element.406), channel_id=1, source_target_pairs={{0,2},{1,3},{2,0},{3,1},{4,6},{5,7},{6,4},{7,5},{8,10},{9,11},{10,... | collective-permute-start | bytes 1572872 | tf_op jit(solution)/shard_map/gnf0x/ppermute | solution.py:435
  440.1 39.5 %collective-permute-start.56 = (bf16[128,2048]{1,0:T(8,128)(2,1)}, bf16[128,2048]{1,0:T(8,128)(2,1)S(1)}, u32[]{:S(2)}, u32[]{:S(2)}) collective-permute-start(bf16[128,2048]{1,0:T(8,128)(2,1)} %get-tuple-element.405), channel_id=1, source_target_pairs={{0,1},{1,2},{2,3},{3,0},{4,5},{5,6},{6,7},{7,4},{8,9},{9,10},{10,1... | collective-permute-start | bytes 1572872 | tf_op jit(solution)/shard_map/gnf0x/ppermute | solution.py:435
  543.5 225.5 %reduce-scatter.8.cloned.1.call-start = ((), (), s32[]{:S(2)}) async-start(), calls=%async_computation.10 | async-start | bytes 5242880 | tf_op jit(solution)/shard_map/reduce_scatter | solution.py:622
  578.4 222.3 %reduce-scatter.10.cloned.1.call-start = ((), (), s32[]{:S(2)}) async-start(), calls=%async_computation.11 | async-start | bytes 5242880 | tf_op jit(solution)/shard_map/reduce_scatter | solution.py:622
  694.8 32.5 %collective-permute-start.84 = (bf16[64,2048]{1,0:T(8,128)(2,1)}, bf16[64,2048]{1,0:T(8,128)(2,1)S(1)}, u32[]{:S(2)}, u32[]{:S(2)}) collective-permute-start(bf16[64,2048]{1,0:T(8,128)(2,1)} %get-tuple-element.432), channel_id=1, source_target_pairs={{0,1},{1,2},{2,3},{3,0},{4,5},{5,6},{6,7},{7,4},{8,9},{9,10},{10,1... | collective-permute-start | bytes 786440 | tf_op jit(solution)/shard_map/swapg/ppermute | solution.py:435
  703.2 32.9 %collective-permute-start.82 = (bf16[128,4096]{1,0:T(8,128)(2,1)S(1)}, bf16[128,4096]{1,0:T(8,128)(2,1)}, u32[]{:S(2)}, u32[]{:S(2)}) collective-permute-start(bf16[128,4096]{1,0:T(8,128)(2,1)S(1)} %add_convert_fusion.5), channel_id=1, source_target_pairs={{0,1},{1,2},{2,3},{4,5},{5,6},{6,7},{8,9},{9,10},{10,11},{12,13},{... | collective-permute-start | bytes 3145736 | tf_op jit(solution)/shard_map/gn0x3/ppermute | solution.py:435
  736.1 32.9 %collective-permute-start.88 = (bf16[128,4096]{1,0:T(8,128)(2,1)}, bf16[128,4096]{1,0:T(8,128)(2,1)}, u32[]{:S(2)}, u32[]{:S(2)}) collective-permute-start(bf16[128,4096]{1,0:T(8,128)(2,1)} %get-tuple-element.262), channel_id=1, source_target_pairs={{3,2},{7,6},{11,10},{15,14},{19,18},{23,22},{27,26},{31,30}} | collective-permute-start | bytes 3145736 | tf_op jit(solution)/shard_map/gn1x1/ppermute | solution.py:435
  737.8 31.3 %collective-permute-start.87 = (bf16[128,4096]{1,0:T(8,128)(2,1)}, bf16[128,4096]{1,0:T(8,128)(2,1)}, u32[]{:S(2)}, u32[]{:S(2)}) collective-permute-start(bf16[128,4096]{1,0:T(8,128)(2,1)} %get-tuple-element.263), channel_id=1, source_target_pairs={{0,1},{4,5},{8,9},{12,13},{16,17},{20,21},{24,25},{28,29}} | collective-permute-start | bytes 3145736 | tf_op jit(solution)/shard_map/gn1x1/ppermute | solution.py:435
  769.2 31.5 %collective-permute-start.91 = (bf16[4,4,64,768]{3,2,1,0:T(8,128)(2,1)}, bf16[4,4,64,768]{3,2,1,0:T(8,128)(2,1)}, u32[]{:S(2)}, u32[]{:S(2)}) collective-permute-start(bf16[4,4,64,768]{3,2,1,0:T(8,128)(2,1)} %copy-done.21), channel_id=1, source_target_pairs={{0,4},{4,0},{8,12},{12,8},{16,20},{20,16},{24,28},{28,24},{1,5},{5... | collective-permute-start | bytes 4718600 | tf_op jit(solution)/shard_map/Wqcore/ppermute | solution.py:435
  786.3 43.4 %all-to-all-start.2 = ((bf16[64,8,1024]{2,0,1:T(8,128)(2,1)}), bf16[64,8,1024]{2,0,1:T(8,128)(2,1)}, u32[]{:S(2)}, u32[]{:S(2)}) async-start(bf16[64,8,1024]{2,0,1:T(8,128)(2,1)} %copy.142), calls=%async_computation.7 | async-start | bytes 2097152 | tf_op jit(solution)/shard_map/all_to_all | solution.py:635
  790.5 96.8 %reduce-scatter.12.cloned.1.call-start = ((), (), s32[]{:S(2)}) async-start(), calls=%async_computation.12 | async-start | bytes 1966080 | tf_op jit(solution)/shard_map/reduce_scatter | solution.py:622
  807.4 112.6 %reduce-scatter.14.cloned.1.call-start = ((), (), s32[]{:S(2)}) async-start(), calls=%async_computation.13 | async-start | bytes 1310720 | tf_op jit(solution)/shard_map/reduce_scatter | solution.py:622
  809.5 31.5 %collective-permute-start.95 = (bf16[64,2048]{1,0:T(8,128)(2,1)}, bf16[64,2048]{1,0:T(8,128)(2,1)S(1)}, u32[]{:S(2)}, u32[]{:S(2)}) collective-permute-start(bf16[64,2048]{1,0:T(8,128)(2,1)} %get-tuple-element.427), channel_id=1, source_target_pairs={{0,1},{1,2},{2,3},{3,0},{4,5},{5,6},{6,7},{7,4},{8,9},{9,10},{10,1... | collective-permute-start | bytes 786440 | tf_op jit(solution)/shard_map/swapu/ppermute | solution.py:435
  819.2 33.6 %collective-permute-start.93 = (bf16[128,4096]{1,0:T(8,128)(2,1)}, bf16[128,4096]{1,0:T(8,128)(2,1)}, u32[]{:S(2)}, u32[]{:S(2)}) collective-permute-start(bf16[128,4096]{1,0:T(8,128)(2,1)} %add_convert_fusion.3), channel_id=1, source_target_pairs={{0,1},{1,2},{2,3},{4,5},{5,6},{6,7},{8,9},{9,10},{10,11},{12,13},{... | collective-permute-start | bytes 3145736 | tf_op jit(solution)/shard_map/gn1x3/ppermute | solution.py:435
  845.0 39.3 %all-to-all-start.3 = ((bf16[64,8,1024]{2,0,1:T(8,128)(2,1)}), bf16[64,8,1024]{2,0,1:T(8,128)(2,1)}, u32[]{:S(2)}, u32[]{:S(2)}) async-start(bf16[64,8,1024]{2,0,1:T(8,128)(2,1)} %copy.145), calls=%async_computation.8 | async-start | bytes 2097152 | tf_op jit(solution)/shard_map/all_to_all | solution.py:635
  (302 other events, 4385.9 us)
Sparse Core Ops, SparseCore 0:
  41.8 30.5 all-gather.4
  146.5 91.5 all-gather.6
  543.7 53.3 reduce-scatter.5
  600.1 52.6 reduce-scatter.7
  655.7 52.6 reduce-scatter.9
  807.6 32.5 reduce-scatter.11
  843.3 37.4 reduce-scatter.13
where the time goes:
time: 940 us; the launch traced here: 930 us
  waiting for transfers between devices  288 us (31%)
  starting transfers between devices  236 us (25%)
  Pallas kernels  175 us (19%)
  other arithmetic  103 us (11%)
  local copies, waits for them, and re-layouts  73.7 us (8%)
  matrix products  36.3 us (4%)
  between operations  18.3 us (2%)
    ppermute x104, waiting for transfers between devices, permute(): return lax.ppermute(x, axis, pairs)  279 us
    ppermute x104, starting transfers between devices, permute(): return lax.ppermute(x, axis, pairs)  217 us
    pallas_call x2, Pallas kernels, ffn_both(): pl.pallas_call(ffn_kernel, grid=(length // tm, ff // tf), in_specs=[rows,...  77.2 us
    pallas_call x10, Pallas kernels, weight_grad(): pl.pallas_call(kernel, grid=grid, in_specs=[pl.BlockSpec(memory_space=plt...  74.2 us
    unnamed x436, local copies, waits for them, and re-layouts  30.9 us
    convert_element_type x15, other arithmetic, step(): block = (block.astype(F32) + self.got[way].astype(F32)).astype(block.dtype)  23.7 us
  transfers between devices with their start and end apart: 118, of which 39 were waited for; matrix products, arithmetic and copies ran while one was open for 19% of the time, Pallas kernels for 14%

commit v1 on v0

--- a/solution.py
+++ b/solution.py
@@ -431,24 +431,29 @@
 
 
 def permute(x, axis, pairs):
+    Clock.sent.append(x)
     with jax.named_scope(SCOPE[0]):
         return lax.ppermute(x, axis, pairs)
 
 
 class Clock:
-    before, here = [], []
+    before, here, sent = [], [], []
 
 
 def now(x):
     return tie(x, *Clock.before)
 
 
+def beside(x):
+    return tie(x, *Clock.before, *Clock.sent)
+
+
 def put(*values):
     Clock.here.extend(values)
 
 
 def tick():
-    Clock.before, Clock.here = Clock.here, []
+    Clock.before, Clock.here, Clock.sent = Clock.here, [], []
 
 
 class Gather:
@@ -521,7 +526,7 @@
     x = now(x)
     got = [permute(x, "shard", [(k, (k + t) % n) for k in range(n)]) for t in range(1, n)]
     put(*got)
-    return jnp.concatenate([x] + got)
+    return [x] + got
 
 
 def scatter_direct(x, name):
@@ -564,26 +569,33 @@
     return functools.reduce(lambda a, c: a + c, [part.astype(F32) for part in swap_z(p)])
 
 
-def swapped_rows(name, pieces, hold):
-    n, i = lax.axis_size("shard"), lax.axis_index("shard")
-    size, g = lax.axis_size("grp"), lax.axis_index("grp")
-    rows = pieces[0].shape[0] // size
-    SCOPE[0] = name
-
-    def part(d):
+class SwappedRows:
+    def __init__(self, name, pieces):
+        self.name, self.pieces = name, pieces
+        self.blocks = {0: self.part(lax.axis_index("shard"))}
+
+    def part(self, d):
+        n, size, g = lax.axis_size("shard"), lax.axis_size("grp"), lax.axis_index("grp")
+        rows = self.pieces[0].shape[0] // size
         cut = []
-        for w in pieces:
+        for w in self.pieces:
             cols = w.shape[1] // n
             cut.append(lax.dynamic_slice(w, (g * rows, d * cols), (rows, cols)))
         return jnp.concatenate(cut, axis=1) if len(cut) > 1 else cut[0]
 
-    blocks = [part(i)]
-    for t in range(1, n):
-        block = now(part((i + t) % n))
-        blocks.append(permute(block, "shard", [(k, (k + t) % n) for k in range(n)]))
-    if hold:
-        put(*blocks[1:])
-    return jnp.stack(in_order(blocks))
+    def step(self, *distances):
+        SCOPE[0] = self.name
+        n, i = lax.axis_size("shard"), lax.axis_index("shard")
+        for t in distances:
+            if 0 < t < n:
+                block = now(self.part((i + t) % n))
+                self.blocks[t] = permute(block, "shard", [(k, (k + t) % n) for k in range(n)])
+                put(self.blocks[t])
+
+    def result(self):
+        n = lax.axis_size("shard")
+        self.step(*[t for t in range(1, n) if t not in self.blocks])
+        return jnp.stack(in_order([now(self.blocks[t]) for t in range(n)]))
 
 
 def all_rows(part):
@@ -599,7 +611,7 @@
     def half(self, which, **more):
         (x, y), *rest = self.args[0]
         which = jnp.stack([which]).astype(jnp.int32)
-        return weight_grad([(now(x), y)] + rest, *self.args[1:], which, **more)
+        return weight_grad([(beside(x), y)] + rest, *self.args[1:], which, **more)
 
     def send(self):
         self.sent = self.half(1 - lax.axis_index("grp") % 2)
@@ -625,16 +637,21 @@
 def column_grads(part, widths):
     n, size = lax.axis_size("shard"), lax.axis_size("grp")
     rows = part.shape[1]
-    outs, start = [], 0
+    pieces, start = [], 0
     for group in widths:
         cols = []
         for width in group:
             cols.append(jnp.swapaxes(part[:, :, start : start + width], 0, 1).reshape(rows, n * width))
             start += width
         whole = jnp.concatenate(cols, axis=1) if len(cols) > 1 else cols[0]
-        moved = lax.all_to_all(whole, "grp", 1, 0, tiled=True)
-        moved = jnp.swapaxes(moved.reshape(size // 2, 2, rows, -1), 0, 1).reshape(size * rows, -1)
-        outs.append(moved.astype(F32))
+        pieces.append(whole.reshape(rows, size, -1))
+    moved = jnp.concatenate(pieces, axis=2) if len(pieces) > 1 else pieces[0]
+    moved = lax.all_to_all(moved.reshape(rows, -1), "grp", 1, 0, tiled=True)
+    moved = jnp.swapaxes(moved.reshape(size // 2, 2, rows, -1), 0, 1).reshape(size * rows, -1)
+    outs, start = [], 0
+    for piece in pieces:
+        outs.append(moved[:, start : start + piece.shape[2]].astype(F32))
+        start += piece.shape[2]
     return outs
 
 
@@ -705,13 +722,14 @@
     own = shard * rows + jnp.arange(rows, dtype=jnp.int32)
     gm_own = [jnp.where((own < ends[b, last])[:, None], cotangent[b, 0], 0) for b in range(batches)]
     me = jnp.stack([shard, jnp.int32(n), jnp.int32(rows // QB)]).astype(jnp.int32)
-    Clock.before, Clock.here = [], []
+    Clock.before, Clock.here, Clock.sent = [], [], []
     tok = [Gather(tokens[b, 0], f"tok{b}x") for b in range(batches)]
     cot0 = Gather(gm_own[0], "cot0x")
-    s_qkv = swapped_rows("sqkv", [query_matrix, key_value_matrix[:, :half_kv], key_value_matrix[:, half_kv:]], True)
+    s_qkv = SwappedRows("sqkv", [query_matrix, key_value_matrix[:, :half_kv], key_value_matrix[:, half_kv:]])
+    s_qkv.step(*range(1, n))
     tok[0].step()
     tick()
-    w_qkv = all_rows(s_qkv)
+    w_qkv = all_rows(s_qkv.result())
     small_full = jnp.concatenate(in_order(gather_small(small)), axis=1)
     gain_attn = small_full[0].astype(F32)
     gain_ffn = small_full[1].astype(F32)
@@ -722,7 +740,8 @@
     tok[0].last()
     tick()
     tok[1].step()
-    s_both = swapped_rows("sgu", [gate_matrix, up_matrix], False)
+    s_both = SwappedRows("sgu", [gate_matrix, up_matrix])
+    s_both.step(1)
     pad = jnp.zeros((qw, -rank % 128), BF)
     out_wide = jnp.concatenate([output_matrix, adapter_down_output, pad], axis=1)
     zero = jnp.zeros
@@ -751,7 +770,7 @@
     fq2, fk2 = doubled(query_feature_matrices), doubled(key_feature_matrices)
 
     def attention(b):
-        x = now(tok[b].result()).astype(F32)
+        x = beside(tok[b].result()).astype(F32)
         normed = (x * norm_scale(x) * gain_attn).astype(BF)
         mid = nt(normed, down_maps_t).astype(BF)
         proj = lax.dot_general(w_qkv, normed, (((0,), (1,)), ((), ())), preferred_element_type=F32)
@@ -780,7 +799,7 @@
     def ffn(b, cot):
         k = keep[b]
         nf = k["send"].result()
-        out, back, product, dgate, dup = ffn_both(now(nf), cot, w_both, down_matrix)
+        out, back, product, dgate, dup = ffn_both(beside(nf), cot, w_both, down_matrix)
         put(dup)
         k.update(nf=nf, gm=cot, out=out, back=back, product=product, dgate=dgate, dup=dup)
 
@@ -793,7 +812,7 @@
 
     def attention_back(b):
         k = keep[b]
-        gb = now(k["send"].result())
+        gb = beside(k["send"].result())
         glo = nt(gb, up_output)
         gctx = nt(output_matrix, gb) + nt(adapter_down_output.astype(F32), glo)
         dq, dk, dv, dfq, dfk = attn_bwd(
@@ -804,23 +823,25 @@
         gn = lax.dot_general(dqkv, w_qkv, (((0,), (1,)), ((), ())), preferred_element_type=F32)
         gn = (gn + nn(glm, down_maps_t.astype(F32))).astype(BF)
         put(gn)
-        both = jnp.concatenate([gn, k["out"]], axis=1)
-        k.update(gb=gb, glo=glo, dqkv=dqkv, glm=glm, dfq=dfq, dfk=dfk, gn=Scatter(both, f"gn{b}x"))
+        k.update(gb=gb, glo=glo, dqkv=dqkv, glm=glm, dfq=dfq, dfk=dfk, gn=Scatter(gn, f"gn{b}x"))
 
     def pairs(one, two):
         return [(k[one], k[two]) for k in keep]
 
     tick()
+    tok[1].step()
+    s_both.step(n - 1)
     keep = [attention(0)]
-    tok[1].step()
-    tick()
-    w_both = all_rows(now(s_both))
+    tick()
+    s_both.step(*range(2, n - 1))
     keep[0]["branch"].step()
     tok[1].last()
+    tick()
+    w_both = all_rows(s_both.result())
     keep[0]["branch"].step()
     tick()
+    keep[0]["branch"].last()
     keep.append(attention(1))
-    keep[0]["branch"].last()
     tick()
     after_attention(0)
     keep[0]["send"].step()
@@ -843,18 +864,20 @@
     tick()
     keep[1]["send"].last()
     tick()
+    cot1 = gather_direct(gm_own[1], "cot1x")
     ffn(0, cot0.result())
-    cot1 = gather_direct(gm_own[1], "cot1x")
-    tick()
-    ffn(1, cot1)
+    tick()
     gnf0 = scatter_direct(keep[0]["back"], "gnf0x")
+    ffn(1, jnp.concatenate([now(c) for c in cot1]))
     tick()
     w_g = Halves("Wg", pairs("nf", "dgate"), 0, 0, True)
     w_u = Halves("Wu", pairs("nf", "dup"), 0, 0, True)
     w_d = Halves("Wd", pairs("product", "gm"), 0, 0, False)
     gnf1 = Scatter(keep[1]["back"], "gnf1x")
+    out = [Scatter(k["out"], f"out{b}x") for b, k in enumerate(keep)]
     after_ffn(0, gnf0)
     keep[0]["send"].step()
+    out[0].step()
     w_g.send()
     w_u.send()
     tick()
@@ -870,60 +893,59 @@
     r_g = w_g.finish()
     tick()
     gnf1.last()
+    out[0].step()
     w_d.core()
     attention_back(0)
+    tick()
+    after_ffn(1, gnf1.result())
+    keep[1]["send"].step()
+    out[0].last()
     w_u.keep()
     r_u = w_u.finish()
     tick()
-    after_ffn(1, gnf1.result())
     keep[1]["send"].step()
+    keep[0]["gn"].step()
     w_d.keep()
     r_d = w_d.finish()
-    tick()
-    keep[1]["send"].step()
-    keep[0]["gn"].step()
     tick()
     keep[1]["send"].last()
     keep[0]["gn"].step()
     put(r_g)
     tick()
-    attention_back(1)
     keep[0]["gn"].last()
     t_g = swap_z(r_g.reshape(n, -1, ffq), "swapg")
-    tick()
+    attention_back(1)
     w_q = Halves("Wq", pairs("normed", "dqkv"), 0, 1, True)
     w_o = Halves("Wo", pairs("ctx", "gb"), 1, 0, False)
     w_q.send()
     w_o.send()
+    tick()
     keep[1]["gn"].step()
-    put(r_u)
-    tick()
-    keep[1]["gn"].step()
+    out[1].step()
     w_q.core()
     w_o.core()
-    put(r_d)
-    tick()
-    keep[1]["gn"].last()
-    t_u = swap_z(r_u.reshape(n, -1, ffq), "swapu")
+    put(r_u)
+    tick()
+    keep[1]["gn"].step()
+    out[1].step()
     w_q.keep()
     r_q = w_q.finish()
     w_o.keep()
     r_o = w_o.finish()
-    (grad_gate,) = column_grads(jnp.stack(in_order(t_g)), [[ffq]])
-    tick()
-    (grad_up,) = column_grads(jnp.stack(in_order(t_u)), [[ffq]])
-    t_q = jnp.stack(in_order(swap_z(r_q.reshape(n, -1, qw + 2 * kw), "swapq")))
-    grad_query, grad_kv = column_grads(t_q, [[qw], [kw, kw]])
-    grad_down = r_d.astype(F32)
-    grad_output = r_o.astype(F32)
+    put(r_d)
+    tick()
+    keep[1]["gn"].last()
+    t_u = swap_z(r_u.reshape(n, -1, ffq), "swapu")
+    (grad_gate,) = column_grads(jnp.stack(in_order([beside(t) for t in t_g])), [[ffq]])
+    tick()
+    out[1].last()
+    for k in keep:
+        k["gn_sum"] = now(k["gn"].result())
     for k in keep:
         k["up_out"] = tn(k["lora"], k["gb_own"])
-    output = []
     token_grads = []
     for k in keep:
-        summed = k["gn"].result()
-        output.append((k["hidden"] + summed[:, width:]).astype(BF))
-        back, attn_gain = norm_back(k["x"], gain_attn, summed[:, :width])
+        back, attn_gain = norm_back(k["x"], gain_attn, k["gn_sum"])
         token_grads.append((k["grad_hidden"] + back).astype(BF))
         k.update(attn_gain=attn_gain)
 
@@ -955,6 +977,13 @@
         added("dfq").reshape(-1),
         added("dfk").reshape(-1),
     ]
+    (grad_up,) = column_grads(jnp.stack(in_order([beside(t) for t in t_u])), [[ffq]])
+    tick()
+    t_q = jnp.stack(in_order(swap_z(r_q.reshape(n, -1, qw + 2 * kw), "swapq")))
+    grad_query, grad_kv = column_grads(t_q, [[qw], [kw, kw]])
+    grad_down = r_d.astype(F32)
+    grad_output = r_o.astype(F32)
+    output = [(k["hidden"] + o.result()).astype(BF) for k, o in zip(keep, out)]
     flat = group_sum(jnp.concatenate([lined] + local).astype(BF))
     shapes = [
         (share,),

time: 940 us -> 920 us (0.979)
  waiting for transfers between devices: 288 us -> 259 us
  starting transfers between devices: 236 us -> 251 us
    ppermute x104 -> x116, waiting for transfers between devices: 279 us -> 255 us  [permute(): return lax.ppermute(x, axis, pairs)]
    ppermute x104 -> x116, starting transfers between devices: 217 us -> 230 us  [permute(): return lax.ppermute(x, axis, pairs)]
    convert_element_type x15 -> x21, other arithmetic: 23.7 us -> 31.6 us  [step(): block = (block.astype(F32) + self.got[way].astype(F32)).astype(block.dtype)]
    unnamed x436 -> x506, local copies, waits for them, and re-layouts: 30.9 us -> 25.6 us
  transfers between devices with their start and end apart: 118 -> 129, of which waited for: 39 -> 34; matrix products, arithmetic and copies ran while one was open for 19% -> 18% of each run, Pallas kernels for 14% -> 19%
where the time goes in v1:
time: 920 us; the launch traced here: 907 us
  waiting for transfers between devices  259 us (28%)
  starting transfers between devices  251 us (27%)
  Pallas kernels  176 us (19%)
  other arithmetic  102 us (11%)
  local copies, waits for them, and re-layouts  66.6 us (7%)
  matrix products  32.8 us (4%)
  between operations  18.9 us (2%)
    ppermute x116, waiting for transfers between devices, permute(): return lax.ppermute(x, axis, pairs)  255 us
    ppermute x116, starting transfers between devices, permute(): return lax.ppermute(x, axis, pairs)  230 us
    pallas_call x2, Pallas kernels, ffn_both(): pl.pallas_call(ffn_kernel, grid=(length // tm, ff // tf), in_specs=[rows,...  77.2 us
    pallas_call x10, Pallas kernels, weight_grad(): pl.pallas_call(kernel, grid=grid, in_specs=[pl.BlockSpec(memory_space=plt...  74.5 us
    convert_element_type x21, other arithmetic, step(): block = (block.astype(F32) + self.got[way].astype(F32)).astype(block.dtype)  31.6 us
    unnamed x506, local copies, waits for them, and re-layouts  25.6 us
  transfers between devices with their start and end apart: 129, of which 34 were waited for; matrix products, arithmetic and copies ran while one was open for 18% of the time, Pallas kernels for 19%

profile of v1, /device:TPU:0, one launch (start us, length us, event | category | flops | bytes accessed | tf_op | source)
XLA Modules:
  0.0 906.5 jit_solution(10964172727113008075)
XLA Ops:
  25.5 8.0 collective-permute-done
  64.4 9.9 %collective-permute-done.7 = bf16[128,2048]{1,0:T(8,128)(2,1)S(1)} collective-permute-done((bf16[128,2048]{1,0:T(8,128)(2,1)}, bf16[128,2048]{1,0:T(8,128)(2,1)S(1)}, u32[]{:S(2)}, u32[]{:S(2)}) %collective-permute-start.7) | collective-permute-done | bytes 524320 | tf_op jit(solution)/shard_map/tok0x3/ppermute | solution.py:436
  82.4 19.0 %collective-permute-done.11 = bf16[64,4096]{1,0:T(8,128)(2,1)S(1)} collective-permute-done((bf16[64,4096]{1,0:T(8,128)(2,1)S(1)}, bf16[64,4096]{1,0:T(8,128)(2,1)S(1)}, u32[]{:S(2)}, u32[]{:S(2)}) %collective-permute-start.11) | collective-permute-done | bytes 524320 | tf_op jit(solution)/shard_map/sgu/ppermute | solution.py:436
  122.0 8.5 collective-permute-start.19
  132.8 19.2 %collective-permute-done.18 = bf16[64,4096]{1,0:T(8,128)(2,1)S(1)} collective-permute-done((bf16[64,4096]{1,0:T(8,128)(2,1)S(1)}, bf16[64,4096]{1,0:T(8,128)(2,1)S(1)}, u32[]{:S(2)}, u32[]{:S(2)}) %collective-permute-start.18) | collective-permute-done | bytes 524320 | tf_op jit(solution)/shard_map/sgu/ppermute | solution.py:436
  164.5 8.1 collective-permute-done.23
  218.5 9.4 %collective-permute-done.29 = bf16[128,2048]{1,0:T(8,128)(2,1)S(1)} collective-permute-done((bf16[128,2048]{1,0:T(8,128)(2,1)S(1)}, bf16[128,2048]{1,0:T(8,128)(2,1)S(1)}, u32[]{:S(2)}, u32[]{:S(2)}) %collective-permute-start.29) | collective-permute-done | bytes 524320 | tf_op jit(solution)/shard_map/nf0x2/ppermute | solution.py:436
  259.3 7.8 collective-permute-done.38
  279.7 19.8 %collective-permute-done.44 = bf16[128,2048]{1,0:T(8,128)(2,1)S(1)} collective-permute-done((bf16[128,2048]{1,0:T(8,128)(2,1)S(1)}, bf16[128,2048]{1,0:T(8,128)(2,1)S(1)}, u32[]{:S(2)}, u32[]{:S(2)}) %collective-permute-start.44) | collective-permute-done | bytes 524320 | tf_op jit(solution)/shard_map/cot0x2/ppermute | solution.py:436
  305.2 9.9 %collective-permute-done.48 = bf16[128,2048]{1,0:T(8,128)(2,1)S(1)} collective-permute-done((bf16[128,2048]{1,0:T(8,128)(2,1)S(1)}, bf16[128,2048]{1,0:T(8,128)(2,1)S(1)}, u32[]{:S(2)}, u32[]{:S(2)}) %collective-permute-start.48) | collective-permute-done | bytes 524320 | tf_op jit(solution)/shard_map/cot0x3/ppermute | solution.py:436
  326.6 22.4 %collective-permute-done.50 = bf16[128,2048]{1,0:T(8,128)(2,1)S(1)} collective-permute-done((bf16[128,2048]{1,0:T(8,128)(2,1)S(1)}, bf16[128,2048]{1,0:T(8,128)(2,1)S(1)}, u32[]{:S(2)}, u32[]{:S(2)}) %collective-permute-start.50) | collective-permute-done | bytes 524320 | tf_op jit(solution)/shard_map/nf1x3/ppermute | solution.py:436
  354.6 38.6 %ffn_both.2 = (bf16[512,2048]{1,0:T(8,128)(2,1)}, bf16[512,2048]{1,0:T(8,128)(2,1)}, bf16[512,2048]{1,0:T(8,128)(2,1)}, bf16[512,2048]{1,0:T(8,128)(2,1)}, bf16[512,2048]{1,0:T(8,128)(2,1)}) custom-call(bf16[512,2048]{1,0:T(8,128)(2,1)} %pad_maximum_fusion.2.x_ref.refs_0_, bf16[512,2048]{1,0:T(8,128)(2,1)} %pad_maximum_fusion.3.g_ref.refs_1_, ...), custom_call_target="tpu_custom_call" | custom-call | flops 25769803776 | bytes 25165824 | tf_op jit(solution)/shard_map/ffn_both/pallas_call | solution.py:338
  405.6 38.6 %ffn_both.3 = (bf16[512,2048]{1,0:T(8,128)(2,1)}, bf16[512,2048]{1,0:T(8,128)(2,1)}, bf16[512,2048]{1,0:T(8,128)(2,1)}, bf16[512,2048]{1,0:T(8,128)(2,1)}, bf16[512,2048]{1,0:T(8,128)(2,1)}) custom-call(bf16[512,2048]{1,0:T(8,128)(2,1)} %pad_maximum_fusion.5.x_ref.refs_2_, bf16[512,2048]{1,0:T(8,128)(2,1)} %copy-done.86, bf16[2048,4096]{1,0:T(8,128)(2,1)} %bitcast.290, ...), custom_call_target="tpu_custom_call" | custom-call | flops 25769803776 | bytes 25165824 | tf_op jit(solution)/shard_map/ffn_both/pallas_call | solution.py:338
  461.8 8.3 weight_grad.11
  470.1 8.3 weight_grad.10
  483.4 10.4 %weight_grad.12 = bf16[4,2048,256]{2,1,0:T(8,128)(2,1)} custom-call(s32[1]{0:T(128)} %bitcast.34.side_ref, bf16[512,2048]{1,0:T(8,128)(2,1)S(1)} %copy-done.11, bf16[512,2048]{1,0:T(8,128)(2,1)S(1)} %copy-done.7, bf16[512,2048]{1,0:T(8,128)(2,1)} %get-tuple-element.252.refs_2_, bf16[512,2048]{1,0:T(8,128)(2,1)} %copy-done.86), custom_call_target="tpu_custom_call" | custom-call | flops 4294967296 | bytes 4194304 | tf_op jit(solution)/shard_map/weight_grad/pallas_call | solution.py:405
  498.6 9.0 weight_grad.13
  516.2 8.0 collective-permute-done.67
  569.2 8.9 weight_grad.14
  598.1 9.9 %collective-permute-done.78 = bf16[128,2048]{1,0:T(8,128)(2,1)S(1)} collective-permute-done((bf16[128,2048]{1,0:T(8,128)(2,1)}, bf16[128,2048]{1,0:T(8,128)(2,1)S(1)}, u32[]{:S(2)}, u32[]{:S(2)}) %collective-permute-start.78) | collective-permute-done | bytes 524320 | tf_op jit(solution)/shard_map/gb1x1/ppermute | solution.py:436
  617.6 11.3 %weight_grad.15 = bf16[4,2048,256]{2,1,0:T(8,128)(2,1)} custom-call(s32[1]{0:T(128)} %bitcast.35.side_ref, bf16[512,2048]{1,0:T(8,128)(2,1)S(1)} %copy-done.12, bf16[512,2048]{1,0:T(8,128)(2,1)S(1)} %copy-done.8, bf16[512,2048]{1,0:T(8,128)(2,1)} %get-tuple-element.252.refs_2_, bf16[512,2048]{1,0:T(8,128)(2,1)} %copy-done.86, bf16[4,2048,256]{2,1,0:T(8,128)(2,1)} %copy-done.83), custom_call_target="tpu_custom_call" | custom-call | flops 4294967296 | bytes 4194304 | tf_op jit(solution)/shard_map/weight_grad/pallas_call | solution.py:405
  703.4 9.6 %collective-permute-done.95 = bf16[128,2048]{1,0:T(8,128)(2,1)S(1)} collective-permute-done((bf16[128,2048]{1,0:T(8,128)(2,1)S(1)}, bf16[128,2048]{1,0:T(8,128)(2,1)S(1)}, u32[]{:S(2)}, u32[]{:S(2)}) %collective-permute-start.95) | collective-permute-done | bytes 524320 | tf_op jit(solution)/shard_map/out1x1/ppermute | solution.py:436
  713.1 10.7 %collective-permute-done.93 = bf16[128,2048]{1,0:T(8,128)(2,1)S(1)} collective-permute-done((bf16[128,2048]{1,0:T(8,128)(2,1)S(1)}, bf16[128,2048]{1,0:T(8,128)(2,1)S(1)}, u32[]{:S(2)}, u32[]{:S(2)}) %collective-permute-start.93) | collective-permute-done | bytes 524320 | tf_op jit(solution)/shard_map/gn1x1/ppermute | solution.py:436
  768.9 9.4 %collective-permute-done.101 = bf16[128,2048]{1,0:T(8,128)(2,1)} collective-permute-done((bf16[128,2048]{1,0:T(8,128)(2,1)}, bf16[128,2048]{1,0:T(8,128)(2,1)}, u32[]{:S(2)}, u32[]{:S(2)}) %collective-permute-start.101) | collective-permute-done | bytes 524320 | tf_op jit(solution)/shard_map/out1x2/ppermute | solution.py:436
  (992 shorter events, 564.6 us)
Async XLA Ops:
  7.2 101.9 %all-gather.5.cloned.1.call-start = ((), (), s32[]{:S(2)}) async-start(), calls=%async_computation.13 | async-start | bytes 3538944 | tf_op jit(solution)/shard_map/all_gather | solution.py:603
  40.1 314.5 %all-gather.7.cloned.1.call-start = ((), (), s32[]{:S(2)}) async-start(), calls=%async_computation.14 | async-start | bytes 18874368 | tf_op jit(solution)/shard_map/all_gather | solution.py:603
  121.0 31.1 %collective-permute-start.20 = (bf16[128,2176]{1,0:T(8,128)(2,1)S(1)}, bf16[128,2176]{1,0:T(8,128)(2,1)S(1)}, u32[]{:S(2)}, u32[]{:S(2)}) collective-permute-start(bf16[128,2176]{1,0:T(8,128)(2,1)S(1)} %get-tuple-element.198), channel_id=1, source_target_pairs={{3,2},{7,6},{11,10},{15,14},{19,18},{23,22},{27,26},{31,30}} | collective-permute-start | bytes 1671176 | tf_op jit(solution)/shard_map/br0x1/ppermute | solution.py:436
  155.4 487.9 %reduce-scatter.6.cloned.1.call-start = ((), (), s32[]{:S(2)}) async-start(), calls=%async_computation.8 | async-start | bytes 5242880 | tf_op jit(solution)/shard_map/reduce_scatter | solution.py:634
  349.1 44.1 %collective-permute-start.51 = (bf16[128,2048]{1,0:T(8,128)(2,1)}, bf16[128,2048]{1,0:T(8,128)(2,1)}, u32[]{:S(2)}, u32[]{:S(2)}) collective-permute-start(bf16[128,2048]{1,0:T(8,128)(2,1)} %get-tuple-element.233), channel_id=1, source_target_pairs={{0,1},{1,2},{2,3},{3,0},{4,5},{5,6},{6,7},{7,4},{8,9},{9,10},{10,1... | collective-permute-start | bytes 1572872 | tf_op jit(solution)/shard_map/cot1x/ppermute | solution.py:436
  349.1 44.1 %collective-permute-start.52 = (bf16[128,2048]{1,0:T(8,128)(2,1)}, bf16[128,2048]{1,0:T(8,128)(2,1)}, u32[]{:S(2)}, u32[]{:S(2)}) collective-permute-start(bf16[128,2048]{1,0:T(8,128)(2,1)} %get-tuple-element.233), channel_id=1, source_target_pairs={{0,2},{1,3},{2,0},{3,1},{4,6},{5,7},{6,4},{7,5},{8,10},{9,11},{10,... | collective-permute-start | bytes 1572872 | tf_op jit(solution)/shard_map/cot1x/ppermute | solution.py:436
  349.1 44.1 %collective-permute-start.53 = (bf16[128,2048]{1,0:T(8,128)(2,1)}, bf16[128,2048]{1,0:T(8,128)(2,1)}, u32[]{:S(2)}, u32[]{:S(2)}) collective-permute-start(bf16[128,2048]{1,0:T(8,128)(2,1)} %get-tuple-element.233), channel_id=1, source_target_pairs={{0,3},{1,0},{2,1},{3,2},{4,7},{5,4},{6,5},{7,6},{8,11},{9,8},{10,9... | collective-permute-start | bytes 1572872 | tf_op jit(solution)/shard_map/cot1x/ppermute | solution.py:436
  396.8 48.6 %collective-permute-start.54 = (bf16[128,2048]{1,0:T(8,128)(2,1)}, bf16[128,2048]{1,0:T(8,128)(2,1)}, u32[]{:S(2)}, u32[]{:S(2)}) collective-permute-start(bf16[128,2048]{1,0:T(8,128)(2,1)} %get-tuple-element.470), channel_id=1, source_target_pairs={{0,3},{1,0},{2,1},{3,2},{4,7},{5,4},{6,5},{7,6},{8,11},{9,8},{10,9... | collective-permute-start | bytes 1572872 | tf_op jit(solution)/shard_map/gnf0x/ppermute | solution.py:436
  397.3 48.0 %collective-permute-start.55 = (bf16[128,2048]{1,0:T(8,128)(2,1)}, bf16[128,2048]{1,0:T(8,128)(2,1)}, u32[]{:S(2)}, u32[]{:S(2)}) collective-permute-start(bf16[128,2048]{1,0:T(8,128)(2,1)} %get-tuple-element.469), channel_id=1, source_target_pairs={{0,2},{1,3},{2,0},{3,1},{4,6},{5,7},{6,4},{7,5},{8,10},{9,11},{10,... | collective-permute-start | bytes 1572872 | tf_op jit(solution)/shard_map/gnf0x/ppermute | solution.py:436
  398.8 46.6 %collective-permute-start.56 = (bf16[128,2048]{1,0:T(8,128)(2,1)}, bf16[128,2048]{1,0:T(8,128)(2,1)}, u32[]{:S(2)}, u32[]{:S(2)}) collective-permute-start(bf16[128,2048]{1,0:T(8,128)(2,1)} %get-tuple-element.468), channel_id=1, source_target_pairs={{0,1},{1,2},{2,3},{3,0},{4,5},{5,6},{6,7},{7,4},{8,9},{9,10},{10,1... | collective-permute-start | bytes 1572872 | tf_op jit(solution)/shard_map/gnf0x/ppermute | solution.py:436
  507.6 219.2 %reduce-scatter.8.cloned.1.call-start = ((), (), s32[]{:S(2)}) async-start(), calls=%async_computation.9 | async-start | bytes 5242880 | tf_op jit(solution)/shard_map/reduce_scatter | solution.py:634
  527.3 36.8 %collective-permute-start.75 = (bf16[4,2048,256]{2,1,0:T(8,128)(2,1)}, bf16[4,2048,256]{2,1,0:T(8,128)(2,1)S(1)}, u32[]{:S(2)}, u32[]{:S(2)}) collective-permute-start(bf16[4,2048,256]{2,1,0:T(8,128)(2,1)} %weight_grad.12), channel_id=1, source_target_pairs={{0,4},{4,0},{8,12},{12,8},{16,20},{20,16},{24,28},{28,24},{1,5},{5... | collective-permute-start | bytes 12582920 | tf_op jit(solution)/shard_map/Wdcore/ppermute | solution.py:436
  528.8 35.3 %collective-permute-start.73 = (bf16[128,2048]{1,0:T(8,128)(2,1)}, bf16[128,2048]{1,0:T(8,128)(2,1)}, u32[]{:S(2)}, u32[]{:S(2)}) collective-permute-start(bf16[128,2048]{1,0:T(8,128)(2,1)} %get-tuple-element.518), channel_id=1, source_target_pairs={{0,1},{1,2},{4,5},{5,6},{8,9},{9,10},{12,13},{13,14},{16,17},{17,1... | collective-permute-start | bytes 1572872 | tf_op jit(solution)/shard_map/out0x2/ppermute | solution.py:436
  578.1 200.2 %reduce-scatter.10.cloned.1.call-start = ((), (), s32[]{:S(2)}) async-start(), calls=%async_computation.10 | async-start | bytes 5242880 | tf_op jit(solution)/shard_map/reduce_scatter | solution.py:634
  641.4 227.0 %reduce-scatter.12.cloned.1.call-start = ((), (), s32[]{:S(2)}) async-start(), calls=%async_computation.11 | async-start | bytes 1966080 | tf_op jit(solution)/shard_map/reduce_scatter | solution.py:634
  654.6 42.7 %collective-permute-start.90 = (bf16[64,2048]{1,0:T(8,128)(2,1)}, bf16[64,2048]{1,0:T(8,128)(2,1)S(1)}, u32[]{:S(2)}, u32[]{:S(2)}) collective-permute-start(bf16[64,2048]{1,0:T(8,128)(2,1)} %get-tuple-element.496), channel_id=1, source_target_pairs={{0,1},{1,2},{2,3},{3,0},{4,5},{5,6},{6,7},{7,4},{8,9},{9,10},{10,1... | collective-permute-start | bytes 786440 | tf_op jit(solution)/shard_map/swapg/ppermute | solution.py:436
  654.6 42.7 %collective-permute-start.91 = (bf16[64,2048]{1,0:T(8,128)(2,1)}, bf16[64,2048]{1,0:T(8,128)(2,1)}, u32[]{:S(2)}, u32[]{:S(2)}) collective-permute-start(bf16[64,2048]{1,0:T(8,128)(2,1)} %get-tuple-element.495), channel_id=1, source_target_pairs={{0,2},{1,3},{2,0},{3,1},{4,6},{5,7},{6,4},{7,5},{8,10},{9,11},{10,... | collective-permute-start | bytes 786440 | tf_op jit(solution)/shard_map/swapg/ppermute | solution.py:436
  657.8 39.5 %collective-permute-start.92 = (bf16[64,2048]{1,0:T(8,128)(2,1)}, bf16[64,2048]{1,0:T(8,128)(2,1)}, u32[]{:S(2)}, u32[]{:S(2)}) collective-permute-start(bf16[64,2048]{1,0:T(8,128)(2,1)} %get-tuple-element.494), channel_id=1, source_target_pairs={{0,3},{1,0},{2,1},{3,2},{4,7},{5,4},{6,5},{7,6},{8,11},{9,8},{10,9... | collective-permute-start | bytes 786440 | tf_op jit(solution)/shard_map/swapg/ppermute | solution.py:436
  660.4 37.0 %collective-permute-start.89 = (bf16[128,2048]{1,0:T(8,128)(2,1)}, bf16[128,2048]{1,0:T(8,128)(2,1)S(1)}, u32[]{:S(2)}, u32[]{:S(2)}) collective-permute-start(bf16[128,2048]{1,0:T(8,128)(2,1)} %add_convert_fusion.11), channel_id=1, source_target_pairs={{3,2},{2,1},{1,0},{7,6},{6,5},{5,4},{11,10},{10,9},{9,8},{15,14},{... | collective-permute-start | bytes 1572872 | tf_op jit(solution)/shard_map/gn0x3/ppermute | solution.py:436
  663.8 33.6 %collective-permute-start.88 = (bf16[128,2048]{1,0:T(8,128)(2,1)}, bf16[128,2048]{1,0:T(8,128)(2,1)}, u32[]{:S(2)}, u32[]{:S(2)}) collective-permute-start(bf16[128,2048]{1,0:T(8,128)(2,1)} %add_convert_fusion.12), channel_id=1, source_target_pairs={{0,1},{1,2},{2,3},{4,5},{5,6},{6,7},{8,9},{9,10},{10,11},{12,13},{... | collective-permute-start | bytes 1572872 | tf_op jit(solution)/shard_map/gn0x3/ppermute | solution.py:436
  737.1 156.6 %reduce-scatter.14.cloned.1.call-start = ((), (), s32[]{:S(2)}) async-start(), calls=%async_computation.12 | async-start | bytes 1310720 | tf_op jit(solution)/shard_map/reduce_scatter | solution.py:634
  780.2 30.7 %collective-permute-start.104 = (bf16[128,2048]{1,0:T(8,128)(2,1)}, bf16[128,2048]{1,0:T(8,128)(2,1)}, u32[]{:S(2)}, u32[]{:S(2)}) collective-permute-start(bf16[128,2048]{1,0:T(8,128)(2,1)} %add_convert_fusion.9), channel_id=1, source_target_pairs={{3,2},{2,1},{1,0},{7,6},{6,5},{5,4},{11,10},{10,9},{9,8},{15,14},{... | collective-permute-start | bytes 1572872 | tf_op jit(solution)/shard_map/gn1x3/ppermute | solution.py:436
  802.4 54.3 %all-to-all-start.1 = ((bf16[64,8,1024]{2,0,1:T(8,128)(2,1)}), bf16[64,8,1024]{2,0,1:T(8,128)(2,1)}, u32[]{:S(2)}, u32[]{:S(2)}) async-start(bf16[64,8,1024]{2,0,1:T(8,128)(2,1)} %copy.143), calls=%async_computation.6 | async-start | bytes 2097152 | tf_op jit(solution)/shard_map/all_to_all | solution.py:649
  831.0 37.3 %collective-permute-start.108 = (bf16[128,2048]{1,0:T(8,128)(2,1)}, bf16[128,2048]{1,0:T(8,128)(2,1)}, u32[]{:S(2)}, u32[]{:S(2)}) collective-permute-start(bf16[128,2048]{1,0:T(8,128)(2,1)} %add_convert_fusion.8), channel_id=1, source_target_pairs={{0,1},{1,2},{2,3},{4,5},{5,6},{6,7},{8,9},{9,10},{10,11},{12,13},{... | collective-permute-start | bytes 1572872 | tf_op jit(solution)/shard_map/out1x3/ppermute | solution.py:436
  (348 other events, 4815.3 us)
Sparse Core Ops, SparseCore 0:
  40.2 30.5 all-gather.4
  155.5 90.3 all-gather.6
  507.7 54.9 reduce-scatter.5
  578.2 56.6 reduce-scatter.7
  641.5 56.0 reduce-scatter.9
  737.2 34.2 reduce-scatter.11
  774.6 27.7 reduce-scatter.13

commit v2 on v1

--- a/solution.py
+++ b/solution.py
@@ -479,7 +479,7 @@
 
     def result(self):
         n, i = lax.axis_size("shard"), lax.axis_index("shard")
-        blocks = [jnp.where(i >= t, self.ups[t - 1], self.downs[n - t - 1]) for t in range(1, n)]
+        blocks = [jnp.where(i >= t, now(self.ups[t - 1]), now(self.downs[n - t - 1])) for t in range(1, n)]
         return jnp.concatenate([self.x] + blocks)
 
 
@@ -629,7 +629,7 @@
 
     def finish(self):
         size = lax.axis_size("grp")
-        flat = self.value.reshape((-1,) + self.value.shape[2:])
+        flat = now(self.value).reshape((-1,) + self.value.shape[2:])
         alike = [[k for k in range(size) if k % 2 == c] for c in range(2)]
         return lax.psum_scatter(flat, "grp", scatter_dimension=0, axis_index_groups=alike, tiled=True)
 
@@ -863,7 +863,6 @@
     cot0.last()
     tick()
     keep[1]["send"].last()
-    tick()
     cot1 = gather_direct(gm_own[1], "cot1x")
     ffn(0, cot0.result())
     tick()
@@ -890,8 +889,8 @@
     gnf1.step()
     w_u.core()
     w_g.keep()
+    tick()
     r_g = w_g.finish()
-    tick()
     gnf1.last()
     out[0].step()
     w_d.core()
@@ -901,13 +900,13 @@
     keep[1]["send"].step()
     out[0].last()
     w_u.keep()
+    tick()
     r_u = w_u.finish()
-    tick()
     keep[1]["send"].step()
     keep[0]["gn"].step()
     w_d.keep()
+    tick()
     r_d = w_d.finish()
-    tick()
     keep[1]["send"].last()
     keep[0]["gn"].step()
     put(r_g)
@@ -929,15 +928,16 @@
     keep[1]["gn"].step()
     out[1].step()
     w_q.keep()
+    w_o.keep()
+    put(r_d)
+    tick()
     r_q = w_q.finish()
-    w_o.keep()
     r_o = w_o.finish()
-    put(r_d)
-    tick()
     keep[1]["gn"].last()
     t_u = swap_z(r_u.reshape(n, -1, ffq), "swapu")
-    (grad_gate,) = column_grads(jnp.stack(in_order([beside(t) for t in t_g])), [[ffq]])
-    tick()
+    (grad_gate,) = column_grads(jnp.stack(in_order([now(t) for t in t_g])), [[ffq]])
+    tick()
+    (grad_up,) = column_grads(jnp.stack(in_order([now(t) for t in t_u])), [[ffq]])
     out[1].last()
     for k in keep:
         k["gn_sum"] = now(k["gn"].result())
@@ -977,8 +977,6 @@
         added("dfq").reshape(-1),
         added("dfk").reshape(-1),
     ]
-    (grad_up,) = column_grads(jnp.stack(in_order([beside(t) for t in t_u])), [[ffq]])
-    tick()
     t_q = jnp.stack(in_order(swap_z(r_q.reshape(n, -1, qw + 2 * kw), "swapq")))
     grad_query, grad_kv = column_grads(t_q, [[qw], [kw, kw]])
     grad_down = r_d.astype(F32)

time: 920 us -> 910 us (0.989)
  waiting for transfers between devices: 259 us -> 218 us
  starting transfers between devices: 251 us -> 269 us
    ppermute x116, waiting for transfers between devices: 255 us -> 213 us  [permute(): return lax.ppermute(x, axis, pairs)]
    ppermute x116, starting transfers between devices: 230 us -> 254 us  [permute(): return lax.ppermute(x, axis, pairs)]
    unnamed x506 -> x518, local copies, waits for them, and re-layouts: 25.6 us -> 26.1 us
  transfers between devices with their start and end apart: 129 -> 129, of which waited for: 34 -> 32; matrix products, arithmetic and copies ran while one was open for 18% -> 20% of each run, Pallas kernels for 19% -> 20%
where the time goes in v2:
time: 910 us; the launch traced here: 896 us
  starting transfers between devices  269 us (30%)
  waiting for transfers between devices  218 us (24%)
  Pallas kernels  178 us (20%)
  other arithmetic  107 us (12%)
  local copies, waits for them, and re-layouts  70.8 us (8%)
  matrix products  34.8 us (4%)
  between operations  18.8 us (2%)
    ppermute x116, starting transfers between devices, permute(): return lax.ppermute(x, axis, pairs)  254 us
    ppermute x116, waiting for transfers between devices, permute(): return lax.ppermute(x, axis, pairs)  213 us
    pallas_call x2, Pallas kernels, ffn_both(): pl.pallas_call(ffn_kernel, grid=(length // tm, ff // tf), in_specs=[rows,...  77.2 us
    pallas_call x10, Pallas kernels, weight_grad(): pl.pallas_call(kernel, grid=grid, in_specs=[pl.BlockSpec(memory_space=plt...  76.3 us
    convert_element_type x21, other arithmetic, step(): block = (block.astype(F32) + self.got[way].astype(F32)).astype(block.dtype)  29.3 us
    unnamed x518, local copies, waits for them, and re-layouts  26.1 us
    select_n x21, other arithmetic, result(): jnp.where(i >= t, now(self.ups[t - 1]), now(self.downs[n - t - 1]))  18.2 us
  transfers between devices with their start and end apart: 129, of which 32 were waited for; matrix products, arithmetic and copies ran while one was open for 20% of the time, Pallas kernels for 20%

profile of v2, /device:TPU:0, one launch (start us, length us, event | category | flops | bytes accessed | tf_op | source)
XLA Modules:
  0.0 895.9 jit_solution(9498798022387551139)
XLA Ops:
  24.8 8.7 collective-permute-done
  47.2 9.2 %collective-permute-done.6 = bf16[128,2048]{1,0:T(8,128)(2,1)} collective-permute-done((bf16[128,2048]{1,0:T(8,128)(2,1)}, bf16[128,2048]{1,0:T(8,128)(2,1)}, u32[]{:S(2)}, u32[]{:S(2)}) %collective-permute-start.6) | collective-permute-done | bytes 524320 | tf_op jit(solution)/shard_map/tok0x2/ppermute | solution.py:436
  79.6 15.1 %collective-permute-done.11 = bf16[64,4096]{1,0:T(8,128)(2,1)S(1)} collective-permute-done((bf16[64,4096]{1,0:T(8,128)(2,1)}, bf16[64,4096]{1,0:T(8,128)(2,1)S(1)}, u32[]{:S(2)}, u32[]{:S(2)}) %collective-permute-start.11) | collective-permute-done | bytes 524320 | tf_op jit(solution)/shard_map/sgu/ppermute | solution.py:436
  94.6 10.7 %collective-permute-start.17 = (bf16[64,4096]{1,0:T(8,128)(2,1)}, bf16[64,4096]{1,0:T(8,128)(2,1)}, u32[]{:S(2)}, u32[]{:S(2)}) collective-permute-start(bf16[64,4096]{1,0:T(8,128)(2,1)} %pad_maximum_fusion.9), channel_id=1, source_target_pairs={{0,3},{1,0},{2,1},{3,2},{4,7},{5,4},{6,5},{7,6},{8,11},{9,8},{10,9... | collective-permute-start | bytes 1572872 | tf_op jit(solution)/shard_map/sgu/ppermute | solution.py:436
  135.4 11.3 %collective-permute-done.22 = bf16[128,2048]{1,0:T(8,128)(2,1)S(1)} collective-permute-done((bf16[128,2048]{1,0:T(8,128)(2,1)}, bf16[128,2048]{1,0:T(8,128)(2,1)S(1)}, u32[]{:S(2)}, u32[]{:S(2)}) %collective-permute-start.22) | collective-permute-done | bytes 524320 | tf_op jit(solution)/shard_map/tok1x3/ppermute | solution.py:436
  160.6 11.8 %collective-permute-done.23 = bf16[128,2176]{1,0:T(8,128)(2,1)S(1)} collective-permute-done((bf16[128,2176]{1,0:T(8,128)(2,1)S(1)}, bf16[128,2176]{1,0:T(8,128)(2,1)S(1)}, u32[]{:S(2)}, u32[]{:S(2)}) %collective-permute-start.23) | collective-permute-done | bytes 557088 | tf_op jit(solution)/shard_map/br0x2/ppermute | solution.py:436
  218.0 14.1 %collective-permute-done.30 = bf16[128,2048]{1,0:T(8,128)(2,1)S(1)} collective-permute-done((bf16[128,2048]{1,0:T(8,128)(2,1)S(1)}, bf16[128,2048]{1,0:T(8,128)(2,1)S(1)}, u32[]{:S(2)}, u32[]{:S(2)}) %collective-permute-start.30) | collective-permute-done | bytes 524320 | tf_op jit(solution)/shard_map/nf0x2/ppermute | solution.py:436
  239.0 13.9 %collective-permute-done.34 = bf16[128,2048]{1,0:T(8,128)(2,1)S(1)} collective-permute-done((bf16[128,2048]{1,0:T(8,128)(2,1)S(1)}, bf16[128,2048]{1,0:T(8,128)(2,1)S(1)}, u32[]{:S(2)}, u32[]{:S(2)}) %collective-permute-start.34) | collective-permute-done | bytes 524320 | tf_op jit(solution)/shard_map/nf0x3/ppermute | solution.py:436
  270.7 13.2 %collective-permute-done.40 = bf16[128,2048]{1,0:T(8,128)(2,1)S(1)} collective-permute-done((bf16[128,2048]{1,0:T(8,128)(2,1)S(1)}, bf16[128,2048]{1,0:T(8,128)(2,1)S(1)}, u32[]{:S(2)}, u32[]{:S(2)}) %collective-permute-start.40) | collective-permute-done | bytes 524320 | tf_op jit(solution)/shard_map/cot0x1/ppermute | solution.py:436
  288.4 10.4 %collective-permute-start.41 = (bf16[128,2048]{1,0:T(8,128)(2,1)S(1)}, bf16[128,2048]{1,0:T(8,128)(2,1)}, u32[]{:S(2)}, u32[]{:S(2)}) collective-permute-start(bf16[128,2048]{1,0:T(8,128)(2,1)S(1)} %multiply_convert_fusion), channel_id=1, source_target_pairs={{0,1},{1,2},{2,3},{4,5},{5,6},{6,7},{8,9},{9,10},{10,11},{12,13},{... | collective-permute-start | bytes 1572872 | tf_op jit(solution)/shard_map/nf1x1/ppermute | solution.py:436
  304.7 7.6 collective-permute-done.42
  317.9 17.6 %collective-permute-done.48 = bf16[128,2048]{1,0:T(8,128)(2,1)} collective-permute-done((bf16[128,2048]{1,0:T(8,128)(2,1)}, bf16[128,2048]{1,0:T(8,128)(2,1)}, u32[]{:S(2)}, u32[]{:S(2)}) %collective-permute-start.48) | collective-permute-done | bytes 524320 | tf_op jit(solution)/shard_map/cot0x3/ppermute | solution.py:436
  335.6 11.1 %collective-permute-done.46 = bf16[128,2048]{1,0:T(8,128)(2,1)} collective-permute-done((bf16[128,2048]{1,0:T(8,128)(2,1)}, bf16[128,2048]{1,0:T(8,128)(2,1)}, u32[]{:S(2)}, u32[]{:S(2)}) %collective-permute-start.46) | collective-permute-done | bytes 524320 | tf_op jit(solution)/shard_map/nf1x2/ppermute | solution.py:436
  361.2 38.6 %ffn_both.2 = (bf16[512,2048]{1,0:T(8,128)(2,1)}, bf16[512,2048]{1,0:T(8,128)(2,1)}, bf16[512,2048]{1,0:T(8,128)(2,1)}, bf16[512,2048]{1,0:T(8,128)(2,1)}, bf16[512,2048]{1,0:T(8,128)(2,1)}) custom-call(bf16[512,2048]{1,0:T(8,128)(2,1)} %pad_maximum_fusion.2.x_ref.refs_0_, bf16[512,2048]{1,0:T(8,128)(2,1)} %pad_maximum_fusion.3.g_ref.refs_1_, ...), custom_call_target="tpu_custom_call" | custom-call | flops 25769803776 | bytes 25165824 | tf_op jit(solution)/shard_map/ffn_both/pallas_call | solution.py:338
  416.1 38.6 %ffn_both.3 = (bf16[512,2048]{1,0:T(8,128)(2,1)}, bf16[512,2048]{1,0:T(8,128)(2,1)}, bf16[512,2048]{1,0:T(8,128)(2,1)}, bf16[512,2048]{1,0:T(8,128)(2,1)}, bf16[512,2048]{1,0:T(8,128)(2,1)}) custom-call(bf16[512,2048]{1,0:T(8,128)(2,1)} %pad_maximum_fusion.5.x_ref.refs_2_, bf16[512,2048]{1,0:T(8,128)(2,1)} %copy-done.85, bf16[2048,4096]{1,0:T(8,128)(2,1)} %bitcast.290, ...), custom_call_target="tpu_custom_call" | custom-call | flops 25769803776 | bytes 25165824 | tf_op jit(solution)/shard_map/ffn_both/pallas_call | solution.py:338
  472.6 8.3 weight_grad.11
  480.9 8.3 weight_grad.10
  499.1 10.4 %weight_grad.12 = bf16[4,2048,256]{2,1,0:T(8,128)(2,1)} custom-call(s32[1]{0:T(128)} %bitcast.34.side_ref, bf16[512,2048]{1,0:T(8,128)(2,1)S(1)} %copy-done.11, bf16[512,2048]{1,0:T(8,128)(2,1)S(1)} %copy-done.7, bf16[512,2048]{1,0:T(8,128)(2,1)} %get-tuple-element.329.refs_2_, bf16[512,2048]{1,0:T(8,128)(2,1)} %copy-done.85), custom_call_target="tpu_custom_call" | custom-call | flops 4294967296 | bytes 4194304 | tf_op jit(solution)/shard_map/weight_grad/pallas_call | solution.py:405
  523.5 8.9 weight_grad.13
  536.2 9.6 %collective-permute-start.73 = (bf16[128,2048]{1,0:T(8,128)(2,1)}, bf16[128,2048]{1,0:T(8,128)(2,1)}, u32[]{:S(2)}, u32[]{:S(2)}) collective-permute-start(bf16[128,2048]{1,0:T(8,128)(2,1)} %get-tuple-element.612), channel_id=1, source_target_pairs={{0,1},{1,2},{4,5},{5,6},{8,9},{9,10},{12,13},{13,14},{16,17},{17,1... | collective-permute-start | bytes 1572872 | tf_op jit(solution)/shard_map/out0x2/ppermute | solution.py:436
  594.3 8.9 weight_grad.14
  603.3 8.1 collective-permute-done.78
  624.3 11.3 %weight_grad.15 = bf16[4,2048,256]{2,1,0:T(8,128)(2,1)} custom-call(s32[1]{0:T(128)} %bitcast.35.side_ref, bf16[512,2048]{1,0:T(8,128)(2,1)S(1)} %copy-done.12, bf16[512,2048]{1,0:T(8,128)(2,1)S(1)} %copy-done.8, bf16[512,2048]{1,0:T(8,128)(2,1)} %get-tuple-element.329.refs_2_, bf16[512,2048]{1,0:T(8,128)(2,1)} %copy-done.85, ...), custom_call_target="tpu_custom_call" | custom-call | flops 4294967296 | bytes 4194304 | tf_op jit(solution)/shard_map/weight_grad/pallas_call | solution.py:405
  724.1 10.4 %collective-permute-done.93 = bf16[128,2048]{1,0:T(8,128)(2,1)} collective-permute-done((bf16[128,2048]{1,0:T(8,128)(2,1)}, bf16[128,2048]{1,0:T(8,128)(2,1)}, u32[]{:S(2)}, u32[]{:S(2)}) %collective-permute-start.93) | collective-permute-done | bytes 524320 | tf_op jit(solution)/shard_map/gn1x1/ppermute | solution.py:436
  (1004 shorter events, 561.1 us)
Async XLA Ops:
  7.2 107.9 %all-gather.5.cloned.1.call-start = ((), (), s32[]{:S(2)}) async-start(), calls=%async_computation.13 | async-start | bytes 3538944 | tf_op jit(solution)/shard_map/all_gather | solution.py:603
  40.1 321.1 %all-gather.7.cloned.1.call-start = ((), (), s32[]{:S(2)}) async-start(), calls=%async_computation.14 | async-start | bytes 18874368 | tf_op jit(solution)/shard_map/all_gather | solution.py:603
  156.4 503.2 %reduce-scatter.6.cloned.1.call-start = ((), (), s32[]{:S(2)}) async-start(), calls=%async_computation.8 | async-start | bytes 5242880 | tf_op jit(solution)/shard_map/reduce_scatter | solution.py:634
  346.7 53.1 %collective-permute-start.51 = (bf16[128,2048]{1,0:T(8,128)(2,1)}, bf16[128,2048]{1,0:T(8,128)(2,1)}, u32[]{:S(2)}, u32[]{:S(2)}) collective-permute-start(bf16[128,2048]{1,0:T(8,128)(2,1)} %get-tuple-element.310), channel_id=1, source_target_pairs={{0,1},{1,2},{2,3},{3,0},{4,5},{5,6},{6,7},{7,4},{8,9},{9,10},{10,1... | collective-permute-start | bytes 1572872 | tf_op jit(solution)/shard_map/cot1x/ppermute | solution.py:436
  346.7 53.1 %collective-permute-start.52 = (bf16[128,2048]{1,0:T(8,128)(2,1)}, bf16[128,2048]{1,0:T(8,128)(2,1)}, u32[]{:S(2)}, u32[]{:S(2)}) collective-permute-start(bf16[128,2048]{1,0:T(8,128)(2,1)} %get-tuple-element.310), channel_id=1, source_target_pairs={{0,2},{1,3},{2,0},{3,1},{4,6},{5,7},{6,4},{7,5},{8,10},{9,11},{10,... | collective-permute-start | bytes 1572872 | tf_op jit(solution)/shard_map/cot1x/ppermute | solution.py:436
  349.0 50.9 %collective-permute-start.53 = (bf16[128,2048]{1,0:T(8,128)(2,1)}, bf16[128,2048]{1,0:T(8,128)(2,1)}, u32[]{:S(2)}, u32[]{:S(2)}) collective-permute-start(bf16[128,2048]{1,0:T(8,128)(2,1)} %get-tuple-element.310), channel_id=1, source_target_pairs={{0,3},{1,0},{2,1},{3,2},{4,7},{5,4},{6,5},{7,6},{8,11},{9,8},{10,9... | collective-permute-start | bytes 1572872 | tf_op jit(solution)/shard_map/cot1x/ppermute | solution.py:436
  350.5 49.3 %collective-permute-start.50 = (bf16[128,2048]{1,0:T(8,128)(2,1)}, bf16[128,2048]{1,0:T(8,128)(2,1)}, u32[]{:S(2)}, u32[]{:S(2)}) collective-permute-start(bf16[128,2048]{1,0:T(8,128)(2,1)} %collective-permute-done.46), channel_id=1, source_target_pairs={{1,0},{5,4},{9,8},{13,12},{17,16},{21,20},{25,24},{29,28}} | collective-permute-start | bytes 1572872 | tf_op jit(solution)/shard_map/nf1x3/ppermute | solution.py:436
  351.8 48.1 %collective-permute-start.49 = (bf16[128,2048]{1,0:T(8,128)(2,1)}, bf16[128,2048]{1,0:T(8,128)(2,1)}, u32[]{:S(2)}, u32[]{:S(2)}) collective-permute-start(bf16[128,2048]{1,0:T(8,128)(2,1)} %collective-permute-done.45), channel_id=1, source_target_pairs={{2,3},{6,7},{10,11},{14,15},{18,19},{22,23},{26,27},{30,31}} | collective-permute-start | bytes 1572872 | tf_op jit(solution)/shard_map/nf1x3/ppermute | solution.py:436
  402.6 53.1 %collective-permute-start.54 = (bf16[128,2048]{1,0:T(8,128)(2,1)}, bf16[128,2048]{1,0:T(8,128)(2,1)S(1)}, u32[]{:S(2)}, u32[]{:S(2)}) collective-permute-start(bf16[128,2048]{1,0:T(8,128)(2,1)} %get-tuple-element.564), channel_id=1, source_target_pairs={{0,3},{1,0},{2,1},{3,2},{4,7},{5,4},{6,5},{7,6},{8,11},{9,8},{10,9... | collective-permute-start | bytes 1572872 | tf_op jit(solution)/shard_map/gnf0x/ppermute | solution.py:436
  403.1 52.6 %collective-permute-start.55 = (bf16[128,2048]{1,0:T(8,128)(2,1)}, bf16[128,2048]{1,0:T(8,128)(2,1)}, u32[]{:S(2)}, u32[]{:S(2)}) collective-permute-start(bf16[128,2048]{1,0:T(8,128)(2,1)} %get-tuple-element.563), channel_id=1, source_target_pairs={{0,2},{1,3},{2,0},{3,1},{4,6},{5,7},{6,4},{7,5},{8,10},{9,11},{10,... | collective-permute-start | bytes 1572872 | tf_op jit(solution)/shard_map/gnf0x/ppermute | solution.py:436
  406.4 49.3 %collective-permute-start.56 = (bf16[128,2048]{1,0:T(8,128)(2,1)}, bf16[128,2048]{1,0:T(8,128)(2,1)}, u32[]{:S(2)}, u32[]{:S(2)}) collective-permute-start(bf16[128,2048]{1,0:T(8,128)(2,1)} %get-tuple-element.562), channel_id=1, source_target_pairs={{0,1},{1,2},{2,3},{3,0},{4,5},{5,6},{6,7},{7,4},{8,9},{9,10},{10,1... | collective-permute-start | bytes 1572872 | tf_op jit(solution)/shard_map/gnf0x/ppermute | solution.py:436
  533.4 44.6 %collective-permute-start.75 = (bf16[4,2048,256]{2,1,0:T(8,128)(2,1)}, bf16[4,2048,256]{2,1,0:T(8,128)(2,1)}, u32[]{:S(2)}, u32[]{:S(2)}) collective-permute-start(bf16[4,2048,256]{2,1,0:T(8,128)(2,1)} %weight_grad.12), channel_id=1, source_target_pairs={{0,4},{4,0},{8,12},{12,8},{16,20},{20,16},{24,28},{28,24},{1,5},{5... | collective-permute-start | bytes 12582920 | tf_op jit(solution)/shard_map/Wdcore/ppermute | solution.py:436
  533.5 201.1 %reduce-scatter.8.cloned.1.call-start = ((), (), s32[]{:S(2)}) async-start(), calls=%async_computation.9 | async-start | bytes 5242880 | tf_op jit(solution)/shard_map/reduce_scatter | solution.py:634
  536.2 41.8 %collective-permute-start.73 = (bf16[128,2048]{1,0:T(8,128)(2,1)}, bf16[128,2048]{1,0:T(8,128)(2,1)}, u32[]{:S(2)}, u32[]{:S(2)}) collective-permute-start(bf16[128,2048]{1,0:T(8,128)(2,1)} %get-tuple-element.612), channel_id=1, source_target_pairs={{0,1},{1,2},{4,5},{5,6},{8,9},{9,10},{12,13},{13,14},{16,17},{17,1... | collective-permute-start | bytes 1572872 | tf_op jit(solution)/shard_map/out0x2/ppermute | solution.py:436
  613.0 152.8 %reduce-scatter.10.cloned.1.call-start = ((), (), s32[]{:S(2)}) async-start(), calls=%async_computation.10 | async-start | bytes 5242880 | tf_op jit(solution)/shard_map/reduce_scatter | solution.py:634
  649.9 207.8 %reduce-scatter.12.cloned.1.call-start = ((), (), s32[]{:S(2)}) async-start(), calls=%async_computation.11 | async-start | bytes 1966080 | tf_op jit(solution)/shard_map/reduce_scatter | solution.py:634
  661.9 43.3 %collective-permute-start.90 = (bf16[64,2048]{1,0:T(8,128)(2,1)}, bf16[64,2048]{1,0:T(8,128)(2,1)S(1)}, u32[]{:S(2)}, u32[]{:S(2)}) collective-permute-start(bf16[64,2048]{1,0:T(8,128)(2,1)} %get-tuple-element.590), channel_id=1, source_target_pairs={{0,1},{1,2},{2,3},{3,0},{4,5},{5,6},{6,7},{7,4},{8,9},{9,10},{10,1... | collective-permute-start | bytes 786440 | tf_op jit(solution)/shard_map/swapg/ppermute | solution.py:436
  661.9 43.3 %collective-permute-start.91 = (bf16[64,2048]{1,0:T(8,128)(2,1)}, bf16[64,2048]{1,0:T(8,128)(2,1)}, u32[]{:S(2)}, u32[]{:S(2)}) collective-permute-start(bf16[64,2048]{1,0:T(8,128)(2,1)} %get-tuple-element.589), channel_id=1, source_target_pairs={{0,2},{1,3},{2,0},{3,1},{4,6},{5,7},{6,4},{7,5},{8,10},{9,11},{10,... | collective-permute-start | bytes 786440 | tf_op jit(solution)/shard_map/swapg/ppermute | solution.py:436
  664.6 40.7 %collective-permute-start.92 = (bf16[64,2048]{1,0:T(8,128)(2,1)}, bf16[64,2048]{1,0:T(8,128)(2,1)}, u32[]{:S(2)}, u32[]{:S(2)}) collective-permute-start(bf16[64,2048]{1,0:T(8,128)(2,1)} %get-tuple-element.588), channel_id=1, source_target_pairs={{0,3},{1,0},{2,1},{3,2},{4,7},{5,4},{6,5},{7,6},{8,11},{9,8},{10,9... | collective-permute-start | bytes 786440 | tf_op jit(solution)/shard_map/swapg/ppermute | solution.py:436
  666.9 38.3 %collective-permute-start.89 = (bf16[128,2048]{1,0:T(8,128)(2,1)S(1)}, bf16[128,2048]{1,0:T(8,128)(2,1)S(1)}, u32[]{:S(2)}, u32[]{:S(2)}) collective-permute-start(bf16[128,2048]{1,0:T(8,128)(2,1)S(1)} %add_convert_fusion.11), channel_id=1, source_target_pairs={{3,2},{2,1},{1,0},{7,6},{6,5},{5,4},{11,10},{10,9},{9,8},{15,14},{... | collective-permute-start | bytes 1572872 | tf_op jit(solution)/shard_map/gn0x3/ppermute | solution.py:436
  797.4 48.7 %all-to-all-start.1 = ((bf16[64,8,1024]{2,0,1:T(8,128)(2,1)}), bf16[64,8,1024]{2,0,1:T(8,128)(2,1)}, u32[]{:S(2)}, u32[]{:S(2)}) async-start(bf16[64,8,1024]{2,0,1:T(8,128)(2,1)} %copy.143), calls=%async_computation.6 | async-start | bytes 2097152 | tf_op jit(solution)/shard_map/all_to_all | solution.py:649
  801.8 81.4 %reduce-scatter.14.cloned.1.call-start = ((), (), s32[]{:S(2)}) async-start(), calls=%async_computation.12 | async-start | bytes 1310720 | tf_op jit(solution)/shard_map/reduce_scatter | solution.py:634
  826.9 51.8 %collective-permute-start.108 = (bf16[128,2048]{1,0:T(8,128)(2,1)}, bf16[128,2048]{1,0:T(8,128)(2,1)}, u32[]{:S(2)}, u32[]{:S(2)}) collective-permute-start(bf16[128,2048]{1,0:T(8,128)(2,1)} %add_convert_fusion.8), channel_id=1, source_target_pairs={{0,1},{1,2},{2,3},{4,5},{5,6},{6,7},{8,9},{9,10},{10,11},{12,13},{... | collective-permute-start | bytes 1572872 | tf_op jit(solution)/shard_map/out1x3/ppermute | solution.py:436
  831.1 47.6 %collective-permute-start.109 = (bf16[128,2048]{1,0:T(8,128)(2,1)}, bf16[128,2048]{1,0:T(8,128)(2,1)}, u32[]{:S(2)}, u32[]{:S(2)}) collective-permute-start(bf16[128,2048]{1,0:T(8,128)(2,1)} %add_convert_fusion.7), channel_id=1, source_target_pairs={{3,2},{2,1},{1,0},{7,6},{6,5},{5,4},{11,10},{10,9},{9,8},{15,14},{... | collective-permute-start | bytes 1572872 | tf_op jit(solution)/shard_map/out1x3/ppermute | solution.py:436
  (354 other events, 5230.2 us)
Sparse Core Ops, SparseCore 0:
  40.2 30.5 all-gather.4
  156.6 89.8 all-gather.6
  533.6 57.1 reduce-scatter.5
  613.1 55.0 reduce-scatter.7
  671.0 52.6 reduce-scatter.9
  766.0 32.6 reduce-scatter.11
  805.8 26.4 reduce-scatter.13

commit v3 on v2

--- a/solution.py
+++ b/solution.py
@@ -982,7 +982,7 @@
     grad_down = r_d.astype(F32)
     grad_output = r_o.astype(F32)
     output = [(k["hidden"] + o.result()).astype(BF) for k, o in zip(keep, out)]
-    flat = group_sum(jnp.concatenate([lined] + local).astype(BF))
+    flat = group_sum(beside(jnp.concatenate([lined] + local).astype(BF)))
     shapes = [
         (share,),
         (share,),

time: 910 us -> 902 us (level)
    unnamed x518 -> x508, local copies, waits for them, and re-layouts: 26.1 us -> 25.5 us
  transfers between devices with their start and end apart: 129 -> 129, of which waited for: 32 -> 32; matrix products, arithmetic and copies ran while one was open for 20% -> 19% of each run, Pallas kernels for 20% -> 20%
where the time goes in v3:
time: 902 us; the launch traced here: 887 us
  starting transfers between devices  269 us (30%)
  waiting for transfers between devices  217 us (24%)
  Pallas kernels  177 us (20%)
  other arithmetic  102 us (11%)
  local copies, waits for them, and re-layouts  68.1 us (8%)
  matrix products  34.8 us (4%)
  between operations  18.9 us (2%)
    ppermute x116, starting transfers between devices, permute(): return lax.ppermute(x, axis, pairs)  253 us
    ppermute x116, waiting for transfers between devices, permute(): return lax.ppermute(x, axis, pairs)  208 us
    pallas_call x2, Pallas kernels, ffn_both(): pl.pallas_call(ffn_kernel, grid=(length // tm, ff // tf), in_specs=[rows,...  77.2 us
    pallas_call x10, Pallas kernels, weight_grad(): pl.pallas_call(kernel, grid=grid, in_specs=[pl.BlockSpec(memory_space=plt...  76.3 us
    convert_element_type x21, other arithmetic, step(): block = (block.astype(F32) + self.got[way].astype(F32)).astype(block.dtype)  29.4 us
    unnamed x508, local copies, waits for them, and re-layouts  25.5 us
    select_n x21, other arithmetic, result(): jnp.where(i >= t, now(self.ups[t - 1]), now(self.downs[n - t - 1]))  18.2 us
  transfers between devices with their start and end apart: 129, of which 32 were waited for; matrix products, arithmetic and copies ran while one was open for 19% of the time, Pallas kernels for 20%

profile of v3, /device:TPU:0, one launch (start us, length us, event | category | flops | bytes accessed | tf_op | source)
XLA Modules:
  0.0 887.4 jit_solution(255201035841976843)
XLA Ops:
  24.8 8.6 collective-permute-done
  47.2 9.2 %collective-permute-done.6 = bf16[128,2048]{1,0:T(8,128)(2,1)} collective-permute-done((bf16[128,2048]{1,0:T(8,128)(2,1)}, bf16[128,2048]{1,0:T(8,128)(2,1)}, u32[]{:S(2)}, u32[]{:S(2)}) %collective-permute-start.6) | collective-permute-done | bytes 524320 | tf_op jit(solution)/shard_map/tok0x2/ppermute | solution.py:436
  79.6 15.1 %collective-permute-done.11 = bf16[64,4096]{1,0:T(8,128)(2,1)S(1)} collective-permute-done((bf16[64,4096]{1,0:T(8,128)(2,1)}, bf16[64,4096]{1,0:T(8,128)(2,1)S(1)}, u32[]{:S(2)}, u32[]{:S(2)}) %collective-permute-start.11) | collective-permute-done | bytes 524320 | tf_op jit(solution)/shard_map/sgu/ppermute | solution.py:436
  94.6 10.7 %collective-permute-start.17 = (bf16[64,4096]{1,0:T(8,128)(2,1)}, bf16[64,4096]{1,0:T(8,128)(2,1)}, u32[]{:S(2)}, u32[]{:S(2)}) collective-permute-start(bf16[64,4096]{1,0:T(8,128)(2,1)} %pad_maximum_fusion.9), channel_id=1, source_target_pairs={{0,3},{1,0},{2,1},{3,2},{4,7},{5,4},{6,5},{7,6},{8,11},{9,8},{10,9... | collective-permute-start | bytes 1572872 | tf_op jit(solution)/shard_map/sgu/ppermute | solution.py:436
  135.4 11.3 %collective-permute-done.22 = bf16[128,2048]{1,0:T(8,128)(2,1)S(1)} collective-permute-done((bf16[128,2048]{1,0:T(8,128)(2,1)}, bf16[128,2048]{1,0:T(8,128)(2,1)S(1)}, u32[]{:S(2)}, u32[]{:S(2)}) %collective-permute-start.22) | collective-permute-done | bytes 524320 | tf_op jit(solution)/shard_map/tok1x3/ppermute | solution.py:436
  160.6 11.8 %collective-permute-done.23 = bf16[128,2176]{1,0:T(8,128)(2,1)S(1)} collective-permute-done((bf16[128,2176]{1,0:T(8,128)(2,1)S(1)}, bf16[128,2176]{1,0:T(8,128)(2,1)S(1)}, u32[]{:S(2)}, u32[]{:S(2)}) %collective-permute-start.23) | collective-permute-done | bytes 557088 | tf_op jit(solution)/shard_map/br0x2/ppermute | solution.py:436
  218.0 14.1 %collective-permute-done.30 = bf16[128,2048]{1,0:T(8,128)(2,1)S(1)} collective-permute-done((bf16[128,2048]{1,0:T(8,128)(2,1)S(1)}, bf16[128,2048]{1,0:T(8,128)(2,1)S(1)}, u32[]{:S(2)}, u32[]{:S(2)}) %collective-permute-start.30) | collective-permute-done | bytes 524320 | tf_op jit(solution)/shard_map/nf0x2/ppermute | solution.py:436
  239.0 13.9 %collective-permute-done.34 = bf16[128,2048]{1,0:T(8,128)(2,1)S(1)} collective-permute-done((bf16[128,2048]{1,0:T(8,128)(2,1)S(1)}, bf16[128,2048]{1,0:T(8,128)(2,1)S(1)}, u32[]{:S(2)}, u32[]{:S(2)}) %collective-permute-start.34) | collective-permute-done | bytes 524320 | tf_op jit(solution)/shard_map/nf0x3/ppermute | solution.py:436
  270.7 13.2 %collective-permute-done.40 = bf16[128,2048]{1,0:T(8,128)(2,1)S(1)} collective-permute-done((bf16[128,2048]{1,0:T(8,128)(2,1)S(1)}, bf16[128,2048]{1,0:T(8,128)(2,1)S(1)}, u32[]{:S(2)}, u32[]{:S(2)}) %collective-permute-start.40) | collective-permute-done | bytes 524320 | tf_op jit(solution)/shard_map/cot0x1/ppermute | solution.py:436
  288.4 10.3 %collective-permute-start.41 = (bf16[128,2048]{1,0:T(8,128)(2,1)S(1)}, bf16[128,2048]{1,0:T(8,128)(2,1)}, u32[]{:S(2)}, u32[]{:S(2)}) collective-permute-start(bf16[128,2048]{1,0:T(8,128)(2,1)S(1)} %multiply_convert_fusion), channel_id=1, source_target_pairs={{0,1},{1,2},{2,3},{4,5},{5,6},{6,7},{8,9},{9,10},{10,11},{12,13},{... | collective-permute-start | bytes 1572872 | tf_op jit(solution)/shard_map/nf1x1/ppermute | solution.py:436
  304.7 7.6 collective-permute-done.42
  317.9 17.7 %collective-permute-done.48 = bf16[128,2048]{1,0:T(8,128)(2,1)} collective-permute-done((bf16[128,2048]{1,0:T(8,128)(2,1)}, bf16[128,2048]{1,0:T(8,128)(2,1)}, u32[]{:S(2)}, u32[]{:S(2)}) %collective-permute-start.48) | collective-permute-done | bytes 524320 | tf_op jit(solution)/shard_map/cot0x3/ppermute | solution.py:436
  335.6 11.1 %collective-permute-done.46 = bf16[128,2048]{1,0:T(8,128)(2,1)} collective-permute-done((bf16[128,2048]{1,0:T(8,128)(2,1)}, bf16[128,2048]{1,0:T(8,128)(2,1)}, u32[]{:S(2)}, u32[]{:S(2)}) %collective-permute-start.46) | collective-permute-done | bytes 524320 | tf_op jit(solution)/shard_map/nf1x2/ppermute | solution.py:436
  361.2 38.5 %ffn_both.2 = (bf16[512,2048]{1,0:T(8,128)(2,1)}, bf16[512,2048]{1,0:T(8,128)(2,1)}, bf16[512,2048]{1,0:T(8,128)(2,1)}, bf16[512,2048]{1,0:T(8,128)(2,1)}, bf16[512,2048]{1,0:T(8,128)(2,1)}) custom-call(bf16[512,2048]{1,0:T(8,128)(2,1)} %pad_maximum_fusion.2.x_ref.refs_0_, bf16[512,2048]{1,0:T(8,128)(2,1)} %pad_maximum_fusion.3.g_ref.refs_1_, ...), custom_call_target="tpu_custom_call" | custom-call | flops 25769803776 | bytes 25165824 | tf_op jit(solution)/shard_map/ffn_both/pallas_call | solution.py:338
  416.0 38.6 %ffn_both.3 = (bf16[512,2048]{1,0:T(8,128)(2,1)}, bf16[512,2048]{1,0:T(8,128)(2,1)}, bf16[512,2048]{1,0:T(8,128)(2,1)}, bf16[512,2048]{1,0:T(8,128)(2,1)}, bf16[512,2048]{1,0:T(8,128)(2,1)}) custom-call(bf16[512,2048]{1,0:T(8,128)(2,1)} %pad_maximum_fusion.5.x_ref.refs_2_, bf16[512,2048]{1,0:T(8,128)(2,1)} %copy-done.85, bf16[2048,4096]{1,0:T(8,128)(2,1)} %bitcast.290, ...), custom_call_target="tpu_custom_call" | custom-call | flops 25769803776 | bytes 25165824 | tf_op jit(solution)/shard_map/ffn_both/pallas_call | solution.py:338
  472.5 8.3 weight_grad.11
  480.8 8.3 weight_grad.10
  498.9 10.4 %weight_grad.12 = bf16[4,2048,256]{2,1,0:T(8,128)(2,1)} custom-call(s32[1]{0:T(128)} %bitcast.34.side_ref, bf16[512,2048]{1,0:T(8,128)(2,1)S(1)} %copy-done.11, bf16[512,2048]{1,0:T(8,128)(2,1)S(1)} %copy-done.7, bf16[512,2048]{1,0:T(8,128)(2,1)} %get-tuple-element.330.refs_2_, bf16[512,2048]{1,0:T(8,128)(2,1)} %copy-done.85), custom_call_target="tpu_custom_call" | custom-call | flops 4294967296 | bytes 4194304 | tf_op jit(solution)/shard_map/weight_grad/pallas_call | solution.py:405
  523.3 8.9 %weight_grad.13 = bf16[4,4,64,2048]{3,2,1,0:T(8,128)(2,1)} custom-call(s32[1]{0:T(128)} %bitcast.35.side_ref, bf16[512,2048]{1,0:T(8,128)(2,1)S(1)} %copy-done.5, bf16[512,2048]{1,0:T(8,128)(2,1)S(1)} %copy-done.15, bf16[512,2048]{1,0:T(8,128)(2,1)} %pad_maximum_fusion.5.x_ref.refs_2_, bf16[512,2048]{1,0:T(8,128)(2,1)} %get-tuple-element.322.refs_3_, ...), custom_call_target="tpu_custom_call" | custom-call | flops 4294967296 | bytes 4194304 | tf_op jit(solution)/shard_map/weight_grad/pallas_call | solution.py:405
  536.0 9.7 %collective-permute-start.73 = (bf16[128,2048]{1,0:T(8,128)(2,1)}, bf16[128,2048]{1,0:T(8,128)(2,1)}, u32[]{:S(2)}, u32[]{:S(2)}) collective-permute-start(bf16[128,2048]{1,0:T(8,128)(2,1)} %get-tuple-element.614), channel_id=1, source_target_pairs={{0,1},{1,2},{4,5},{5,6},{8,9},{9,10},{12,13},{13,14},{16,17},{17,1... | collective-permute-start | bytes 1572872 | tf_op jit(solution)/shard_map/out0x2/ppermute | solution.py:436
  594.1 9.0 %weight_grad.14 = bf16[4,4,64,2048]{3,2,1,0:T(8,128)(2,1)} custom-call(s32[1]{0:T(128)} %bitcast.35.side_ref, bf16[512,2048]{1,0:T(8,128)(2,1)S(1)} %copy-done.6, bf16[512,2048]{1,0:T(8,128)(2,1)S(1)} %copy-done.14, bf16[512,2048]{1,0:T(8,128)(2,1)} %pad_maximum_fusion.5.x_ref.refs_2_, bf16[512,2048]{1,0:T(8,128)(2,1)} %get-tuple-element.316.refs_3_, ...), custom_call_target="tpu_custom_call" | custom-call | flops 4294967296 | bytes 4194304 | tf_op jit(solution)/shard_map/weight_grad/pallas_call | solution.py:405
  603.1 8.1 collective-permute-done.78
  624.2 11.3 %weight_grad.15 = bf16[4,2048,256]{2,1,0:T(8,128)(2,1)} custom-call(s32[1]{0:T(128)} %bitcast.35.side_ref, bf16[512,2048]{1,0:T(8,128)(2,1)S(1)} %copy-done.12, bf16[512,2048]{1,0:T(8,128)(2,1)S(1)} %copy-done.8, bf16[512,2048]{1,0:T(8,128)(2,1)} %get-tuple-element.330.refs_2_, bf16[512,2048]{1,0:T(8,128)(2,1)} %copy-done.85, ...), custom_call_target="tpu_custom_call" | custom-call | flops 4294967296 | bytes 4194304 | tf_op jit(solution)/shard_map/weight_grad/pallas_call | solution.py:405
  723.8 10.4 %collective-permute-done.93 = bf16[128,2048]{1,0:T(8,128)(2,1)} collective-permute-done((bf16[128,2048]{1,0:T(8,128)(2,1)}, bf16[128,2048]{1,0:T(8,128)(2,1)}, u32[]{:S(2)}, u32[]{:S(2)}) %collective-permute-start.93) | collective-permute-done | bytes 524320 | tf_op jit(solution)/shard_map/gn1x1/ppermute | solution.py:436
  (994 shorter events, 552.5 us)
Async XLA Ops:
  7.2 107.9 %all-gather.5.cloned.1.call-start = ((), (), s32[]{:S(2)}) async-start(), calls=%async_computation.13 | async-start | bytes 3538944 | tf_op jit(solution)/shard_map/all_gather | solution.py:603
  40.1 321.1 %all-gather.7.cloned.1.call-start = ((), (), s32[]{:S(2)}) async-start(), calls=%async_computation.14 | async-start | bytes 18874368 | tf_op jit(solution)/shard_map/all_gather | solution.py:603
  94.6 32.3 %collective-permute-start.17 = (bf16[64,4096]{1,0:T(8,128)(2,1)}, bf16[64,4096]{1,0:T(8,128)(2,1)}, u32[]{:S(2)}, u32[]{:S(2)}) collective-permute-start(bf16[64,4096]{1,0:T(8,128)(2,1)} %pad_maximum_fusion.9), channel_id=1, source_target_pairs={{0,3},{1,0},{2,1},{3,2},{4,7},{5,4},{6,5},{7,6},{8,11},{9,8},{10,9... | collective-permute-start | bytes 1572872 | tf_op jit(solution)/shard_map/sgu/ppermute | solution.py:436
  156.4 503.0 %reduce-scatter.6.cloned.1.call-start = ((), (), s32[]{:S(2)}) async-start(), calls=%async_computation.8 | async-start | bytes 5242880 | tf_op jit(solution)/shard_map/reduce_scatter | solution.py:634
  346.7 53.0 %collective-permute-start.51 = (bf16[128,2048]{1,0:T(8,128)(2,1)}, bf16[128,2048]{1,0:T(8,128)(2,1)}, u32[]{:S(2)}, u32[]{:S(2)}) collective-permute-start(bf16[128,2048]{1,0:T(8,128)(2,1)} %get-tuple-element.311), channel_id=1, source_target_pairs={{0,1},{1,2},{2,3},{3,0},{4,5},{5,6},{6,7},{7,4},{8,9},{9,10},{10,1... | collective-permute-start | bytes 1572872 | tf_op jit(solution)/shard_map/cot1x/ppermute | solution.py:436
  346.7 53.0 %collective-permute-start.52 = (bf16[128,2048]{1,0:T(8,128)(2,1)}, bf16[128,2048]{1,0:T(8,128)(2,1)}, u32[]{:S(2)}, u32[]{:S(2)}) collective-permute-start(bf16[128,2048]{1,0:T(8,128)(2,1)} %get-tuple-element.311), channel_id=1, source_target_pairs={{0,2},{1,3},{2,0},{3,1},{4,6},{5,7},{6,4},{7,5},{8,10},{9,11},{10,... | collective-permute-start | bytes 1572872 | tf_op jit(solution)/shard_map/cot1x/ppermute | solution.py:436
  348.9 50.8 %collective-permute-start.53 = (bf16[128,2048]{1,0:T(8,128)(2,1)}, bf16[128,2048]{1,0:T(8,128)(2,1)}, u32[]{:S(2)}, u32[]{:S(2)}) collective-permute-start(bf16[128,2048]{1,0:T(8,128)(2,1)} %get-tuple-element.311), channel_id=1, source_target_pairs={{0,3},{1,0},{2,1},{3,2},{4,7},{5,4},{6,5},{7,6},{8,11},{9,8},{10,9... | collective-permute-start | bytes 1572872 | tf_op jit(solution)/shard_map/cot1x/ppermute | solution.py:436
  350.5 49.2 %collective-permute-start.50 = (bf16[128,2048]{1,0:T(8,128)(2,1)}, bf16[128,2048]{1,0:T(8,128)(2,1)}, u32[]{:S(2)}, u32[]{:S(2)}) collective-permute-start(bf16[128,2048]{1,0:T(8,128)(2,1)} %collective-permute-done.46), channel_id=1, source_target_pairs={{1,0},{5,4},{9,8},{13,12},{17,16},{21,20},{25,24},{29,28}} | collective-permute-start | bytes 1572872 | tf_op jit(solution)/shard_map/nf1x3/ppermute | solution.py:436
  351.8 48.0 %collective-permute-start.49 = (bf16[128,2048]{1,0:T(8,128)(2,1)}, bf16[128,2048]{1,0:T(8,128)(2,1)}, u32[]{:S(2)}, u32[]{:S(2)}) collective-permute-start(bf16[128,2048]{1,0:T(8,128)(2,1)} %collective-permute-done.45), channel_id=1, source_target_pairs={{2,3},{6,7},{10,11},{14,15},{18,19},{22,23},{26,27},{30,31}} | collective-permute-start | bytes 1572872 | tf_op jit(solution)/shard_map/nf1x3/ppermute | solution.py:436
  402.4 53.2 %collective-permute-start.54 = (bf16[128,2048]{1,0:T(8,128)(2,1)}, bf16[128,2048]{1,0:T(8,128)(2,1)S(1)}, u32[]{:S(2)}, u32[]{:S(2)}) collective-permute-start(bf16[128,2048]{1,0:T(8,128)(2,1)} %get-tuple-element.566), channel_id=1, source_target_pairs={{0,3},{1,0},{2,1},{3,2},{4,7},{5,4},{6,5},{7,6},{8,11},{9,8},{10,9... | collective-permute-start | bytes 1572872 | tf_op jit(solution)/shard_map/gnf0x/ppermute | solution.py:436
  403.0 52.6 %collective-permute-start.55 = (bf16[128,2048]{1,0:T(8,128)(2,1)}, bf16[128,2048]{1,0:T(8,128)(2,1)}, u32[]{:S(2)}, u32[]{:S(2)}) collective-permute-start(bf16[128,2048]{1,0:T(8,128)(2,1)} %get-tuple-element.565), channel_id=1, source_target_pairs={{0,2},{1,3},{2,0},{3,1},{4,6},{5,7},{6,4},{7,5},{8,10},{9,11},{10,... | collective-permute-start | bytes 1572872 | tf_op jit(solution)/shard_map/gnf0x/ppermute | solution.py:436
  406.3 49.3 %collective-permute-start.56 = (bf16[128,2048]{1,0:T(8,128)(2,1)}, bf16[128,2048]{1,0:T(8,128)(2,1)}, u32[]{:S(2)}, u32[]{:S(2)}) collective-permute-start(bf16[128,2048]{1,0:T(8,128)(2,1)} %get-tuple-element.564), channel_id=1, source_target_pairs={{0,1},{1,2},{2,3},{3,0},{4,5},{5,6},{6,7},{7,4},{8,9},{9,10},{10,1... | collective-permute-start | bytes 1572872 | tf_op jit(solution)/shard_map/gnf0x/ppermute | solution.py:436
  533.2 44.7 %collective-permute-start.75 = (bf16[4,2048,256]{2,1,0:T(8,128)(2,1)}, bf16[4,2048,256]{2,1,0:T(8,128)(2,1)}, u32[]{:S(2)}, u32[]{:S(2)}) collective-permute-start(bf16[4,2048,256]{2,1,0:T(8,128)(2,1)} %weight_grad.12), channel_id=1, source_target_pairs={{0,4},{4,0},{8,12},{12,8},{16,20},{20,16},{24,28},{28,24},{1,5},{5... | collective-permute-start | bytes 12582920 | tf_op jit(solution)/shard_map/Wdcore/ppermute | solution.py:436
  533.2 201.0 %reduce-scatter.8.cloned.1.call-start = ((), (), s32[]{:S(2)}) async-start(), calls=%async_computation.9 | async-start | bytes 5242880 | tf_op jit(solution)/shard_map/reduce_scatter | solution.py:634
  536.0 41.9 %collective-permute-start.73 = (bf16[128,2048]{1,0:T(8,128)(2,1)}, bf16[128,2048]{1,0:T(8,128)(2,1)}, u32[]{:S(2)}, u32[]{:S(2)}) collective-permute-start(bf16[128,2048]{1,0:T(8,128)(2,1)} %get-tuple-element.614), channel_id=1, source_target_pairs={{0,1},{1,2},{4,5},{5,6},{8,9},{9,10},{12,13},{13,14},{16,17},{17,1... | collective-permute-start | bytes 1572872 | tf_op jit(solution)/shard_map/out0x2/ppermute | solution.py:436
  612.9 152.6 %reduce-scatter.10.cloned.1.call-start = ((), (), s32[]{:S(2)}) async-start(), calls=%async_computation.10 | async-start | bytes 5242880 | tf_op jit(solution)/shard_map/reduce_scatter | solution.py:634
  649.7 195.6 %reduce-scatter.12.cloned.1.call-start = ((), (), s32[]{:S(2)}) async-start(), calls=%async_computation.11 | async-start | bytes 1966080 | tf_op jit(solution)/shard_map/reduce_scatter | solution.py:634
  661.7 43.3 %collective-permute-start.90 = (bf16[64,2048]{1,0:T(8,128)(2,1)}, bf16[64,2048]{1,0:T(8,128)(2,1)S(1)}, u32[]{:S(2)}, u32[]{:S(2)}) collective-permute-start(bf16[64,2048]{1,0:T(8,128)(2,1)} %get-tuple-element.592), channel_id=1, source_target_pairs={{0,1},{1,2},{2,3},{3,0},{4,5},{5,6},{6,7},{7,4},{8,9},{9,10},{10,1... | collective-permute-start | bytes 786440 | tf_op jit(solution)/shard_map/swapg/ppermute | solution.py:436
  661.7 43.3 %collective-permute-start.91 = (bf16[64,2048]{1,0:T(8,128)(2,1)}, bf16[64,2048]{1,0:T(8,128)(2,1)}, u32[]{:S(2)}, u32[]{:S(2)}) collective-permute-start(bf16[64,2048]{1,0:T(8,128)(2,1)} %get-tuple-element.591), channel_id=1, source_target_pairs={{0,2},{1,3},{2,0},{3,1},{4,6},{5,7},{6,4},{7,5},{8,10},{9,11},{10,... | collective-permute-start | bytes 786440 | tf_op jit(solution)/shard_map/swapg/ppermute | solution.py:436
  664.4 40.7 %collective-permute-start.92 = (bf16[64,2048]{1,0:T(8,128)(2,1)}, bf16[64,2048]{1,0:T(8,128)(2,1)}, u32[]{:S(2)}, u32[]{:S(2)}) collective-permute-start(bf16[64,2048]{1,0:T(8,128)(2,1)} %get-tuple-element.590), channel_id=1, source_target_pairs={{0,3},{1,0},{2,1},{3,2},{4,7},{5,4},{6,5},{7,6},{8,11},{9,8},{10,9... | collective-permute-start | bytes 786440 | tf_op jit(solution)/shard_map/swapg/ppermute | solution.py:436
  666.7 38.3 %collective-permute-start.89 = (bf16[128,2048]{1,0:T(8,128)(2,1)S(1)}, bf16[128,2048]{1,0:T(8,128)(2,1)S(1)}, u32[]{:S(2)}, u32[]{:S(2)}) collective-permute-start(bf16[128,2048]{1,0:T(8,128)(2,1)S(1)} %add_convert_fusion.11), channel_id=1, source_target_pairs={{3,2},{2,1},{1,0},{7,6},{6,5},{5,4},{11,10},{10,9},{9,8},{15,14},{... | collective-permute-start | bytes 1572872 | tf_op jit(solution)/shard_map/gn0x3/ppermute | solution.py:436
  669.4 35.6 %collective-permute-start.88 = (bf16[128,2048]{1,0:T(8,128)(2,1)S(1)}, bf16[128,2048]{1,0:T(8,128)(2,1)S(1)}, u32[]{:S(2)}, u32[]{:S(2)}) collective-permute-start(bf16[128,2048]{1,0:T(8,128)(2,1)S(1)} %add_convert_fusion.12), channel_id=1, source_target_pairs={{0,1},{1,2},{2,3},{4,5},{5,6},{6,7},{8,9},{9,10},{10,11},{12,13},{... | collective-permute-start | bytes 1572872 | tf_op jit(solution)/shard_map/gn0x3/ppermute | solution.py:436
  796.2 38.0 %all-to-all-start.1 = ((bf16[64,8,1024]{2,0,1:T(8,128)(2,1)}), bf16[64,8,1024]{2,0,1:T(8,128)(2,1)}, u32[]{:S(2)}, u32[]{:S(2)}) async-start(bf16[64,8,1024]{2,0,1:T(8,128)(2,1)} %copy.143), calls=%async_computation.6 | async-start | bytes 2097152 | tf_op jit(solution)/shard_map/all_to_all | solution.py:649
  800.5 54.7 %reduce-scatter.14.cloned.1.call-start = ((), (), s32[]{:S(2)}) async-start(), calls=%async_computation.12 | async-start | bytes 1310720 | tf_op jit(solution)/shard_map/reduce_scatter | solution.py:634
  (349 other events, 5088.5 us)
Sparse Core Ops, SparseCore 0:
  40.2 30.5 all-gather.4
  156.5 89.9 all-gather.6
  533.3 57.2 reduce-scatter.5
  613.0 55.0 reduce-scatter.7
  670.9 52.6 reduce-scatter.9
  765.6 32.6 reduce-scatter.11
  804.5 26.4 reduce-scatter.13
